TPU v7x, 256 devices: a whole 4x4x8 slice. The times are simulated.
256 devices in a mesh: dp: 8 (over y, z_hi), expert: 32 (over x, z_lo, core).
Axes of the slice: x: 4, y: 4, z: 8 (z_hi: 2, z_lo: 4; z = z_hi * 4 + z_lo), core: 2. Of those that a mesh axis runs over, the one named last changes fastest.
Arguments:
- token_blocks: bfloat16 [256, 128, 6144], P('expert', 'dp'), may hold values from -6 to 6
- output_grads: bfloat16 [256, 128, 6144], P('expert', 'dp'), may hold values from -0.1875 to 0.1875
- replica_weights: bfloat16 [32, 3, 144, 6144], P('expert'), as said below
- replica_counts: int32 [8], replicated, may hold values from 1 to 8, as said below
- replica_column: int32 [32], replicated, may hold values from 0 to 31, as said below
- block_dest: int32 [32, 8], replicated, may hold values from 0 to 31, as said below
- block_counts: int32 [32], replicated, may hold values from 3 to 8, as said below
Outputs:
- expert_grads: bfloat16 [8, 3, 144, 6144], P(None, None, 'dp', 'expert')
Inputs may be any that keep to these rules, and one draw needn't show every extreme that they name: `replica_counts`: the replica counts sum to 32. `replica_column`: A permutation of the expert-axis indices; replicas are numbered expert by expert: the first replica_counts[0] replicas belong to expert 0, the next replica_counts[1] to expert 1, and so on. `replica_weights`: replicas of one expert hold equal weights. `block_dest`: the slots of one expert-axis index go to different replicas, and for each k the 32 indices send their k-th slots to different replicas; so a replica receives at most 8 live slots, and some replica receives exactly that many. `block_counts`: slots k below the count are live; the others are ignored.
All inputs are finite; a program needn't handle non-finite values.
Results may differ from a plain program's by a relative error of at most 0.0049.
Values may be sent and summed in bfloat16 or wider, within the bound.
A program may use at most 128 MiB of HBM per device.

v0:
```python
import jax
import jax.numpy as jnp
from jax import lax
from jax.sharding import PartitionSpec as P

EXPERTS = 8


def project_rows(inputs, weights):
    gate_rows = jnp.einsum("md,fd->mf", inputs, weights[0], preferred_element_type=jnp.float32)
    up_rows = jnp.einsum("md,fd->mf", inputs, weights[1], preferred_element_type=jnp.float32)
    return (gate_rows, up_rows)


def local_gradients(inputs, cotangents, gate_rows, up_rows, weights):
    gate_sig = jax.nn.sigmoid(gate_rows)
    activated = gate_rows * gate_sig
    hidden = (activated * up_rows).astype(jnp.bfloat16)
    hidden_grad = jnp.einsum(
        "md,fd->mf", cotangents, weights[2], preferred_element_type=jnp.float32
    )
    gate_grad = (hidden_grad * up_rows * gate_sig * (1.0 + gate_rows * (1.0 - gate_sig))).astype(
        jnp.bfloat16
    )
    up_grad = (hidden_grad * activated).astype(jnp.bfloat16)
    first = jnp.einsum("mf,md->fd", gate_grad, inputs, preferred_element_type=jnp.float32)
    second = jnp.einsum("mf,md->fd", up_grad, inputs, preferred_element_type=jnp.float32)
    third = jnp.einsum("mf,md->fd", hidden, cotangents, preferred_element_type=jnp.float32)
    return jnp.stack([first, second, third])


def on_device(
    token_blocks,
    output_grads,
    replica_weights,
    replica_counts,
    replica_column,
    block_dest,
    block_counts,
):
    columns = lax.axis_size("expert")
    column_here = lax.axis_index("expert")
    slot_count = token_blocks.shape[0]
    width = token_blocks.shape[2]
    column_ids = jnp.arange(columns, dtype=jnp.int32)
    slot_ids = jnp.arange(slot_count, dtype=jnp.int32)
    cumulative = jnp.cumsum(replica_counts)
    replica_expert = jnp.sum((cumulative[None, :] <= column_ids[:, None]).astype(jnp.int32), axis=1)
    placed = (replica_column[:, None] == column_ids[None, :]).astype(jnp.int32)
    column_expert = jnp.sum(placed * replica_expert[:, None], axis=0)
    my_replica = jnp.sum(jnp.where(replica_column == column_here, column_ids, 0))
    own_dest = lax.dynamic_index_in_dim(block_dest, column_here, 0, keepdims=False)
    own_count = lax.dynamic_index_in_dim(block_counts, column_here, 0, keepdims=False)
    dest_column = jnp.sum(
        jnp.where(own_dest[:, None] == column_ids[None, :], replica_column[None, :], 0), axis=1
    )
    send_pick = (
        (dest_column[None, :] == column_ids[:, None]) & (slot_ids[None, :] < own_count)
    ).astype(jnp.bfloat16)
    receive_pick = (
        (block_dest.T == my_replica) & (slot_ids[:, None] < block_counts[None, :])
    ).astype(jnp.bfloat16)
    weights = replica_weights[0]

    def pack_blocks(blocks):
        return jnp.einsum(
            "js,srd->jrd", send_pick, blocks, preferred_element_type=jnp.float32
        ).astype(jnp.bfloat16)

    def unpack_blocks(received):
        placed_rows = jnp.einsum(
            "sj,jrd->srd", receive_pick, received, preferred_element_type=jnp.float32
        )
        return placed_rows.astype(jnp.bfloat16).reshape(-1, width)

    arrived, arrived_grads = (
        lax.all_to_all(
            pack_blocks(token_blocks), "expert", split_axis=0, concat_axis=0, tiled=True
        ),
        lax.all_to_all(
            pack_blocks(output_grads), "expert", split_axis=0, concat_axis=0, tiled=True
        ),
    )
    inputs = unpack_blocks(arrived)
    cotangents = unpack_blocks(arrived_grads)
    gate_rows, up_rows = project_rows(inputs, weights)
    local_grads = local_gradients(inputs, cotangents, gate_rows, up_rows, weights)
    expert_pick = (jnp.arange(EXPERTS, dtype=jnp.int32)[:, None] == column_expert[None, :]).astype(
        jnp.float32
    )
    pieces = lax.all_to_all(local_grads, "expert", split_axis=2, concat_axis=0, tiled=True)
    pieces = pieces.reshape(columns, 3, pieces.shape[1], pieces.shape[2])
    per_expert = jnp.einsum("en,nafd->eafd", expert_pick, pieces, precision=lax.Precision.HIGHEST)
    summed = lax.psum_scatter(per_expert, "dp", scatter_dimension=2, tiled=True)
    return summed.astype(jnp.bfloat16)


def solution(mesh):
    placed = (
        P("expert", "dp", None),
        P("expert", "dp", None),
        P("expert", None, None, None),
        P(),
        P(),
        P(),
        P(),
    )
    return jax.shard_map(
        on_device,
        mesh=mesh,
        in_specs=placed,
        out_specs=P(None, None, "dp", "expert"),
        check_vma=False,
    )
```

profile of v0, /device:TPU:25, one launch (start us, length us, event | category | flops | bytes accessed | tf_op | source)
XLA Modules:
  0.0 1073.4 jit_solution(17897342076074818524)
XLA Ops:
  0.0 1.4 dynamic_slice.9
  1.4 0.6 iota_compare_fusion.6
  2.0 0.9 dynamic-slice_reduce_fusion
  2.9 0.8 select_reduce_fusion.1
  3.7 2.7 convolution_convert_fusion
  6.4 6.1 copy.25
  12.5 9.4 all-to-all-start.1
  21.9 2.7 convolution_convert_fusion.1
  24.5 6.1 copy.21
  30.6 130.7 %all-to-all-done.1 = bf16[32,16,6144]{2,1,0:T(8,128)(2,1)} async-done(((bf16[32,16,6144]{2,1,0:T(8,128)(2,1)}), bf16[32,16,6144]{2,1,0:T(8,128)(2,1)}, u32[]{:S(2)}, u32[]{:S(2)}) %all-to-all-start.1) | async-done | bytes 6291488 | tf_op jit(solution)/shard_map/all_to_all | solution.py:77
  161.3 6.2 all-to-all-start
  167.5 0.6 fusion.32
  168.1 0.7 fusion.22
  168.8 9.5 convolution_convert_fusion.2
  178.3 0.9 copy.27
  179.1 2.1 fusion.4
  181.3 2.1 fusion.6
  183.4 123.2 %all-to-all-done = bf16[32,16,6144]{2,1,0:T(8,128)(2,1)} async-done(((bf16[32,16,6144]{2,1,0:T(8,128)(2,1)}), bf16[32,16,6144]{2,1,0:T(8,128)(2,1)}, u32[]{:S(2)}, u32[]{:S(2)}) %all-to-all-start) | async-done | bytes 6291488 | tf_op jit(solution)/shard_map/all_to_all | solution.py:80
  306.5 9.7 convolution_convert_fusion.3
  316.2 0.9 copy.23
  317.1 2.2 fusion.8
  321.1 4.6 pad_maximum_fusion
  325.7 22.1 %copy.28 = f32[3,144,6144]{1,0,2:T(4,128)} copy(f32[3,144,6144]{2,1,0:T(8,128)} %pad_maximum_fusion) | data formatting | bytes 21233664 | tf_op jit(solution)/shard_map/stack | solution.py:29
  347.8 35.5 %reshape.62 = f32[32,1,82944]{2,1,0:T(1,128)} reshape(f32[6144,3,144]{2,1,0:T(4,128)} %bitcast.52) | data formatting | bytes 21233664
  383.3 6.3 all-to-all-start.2
  391.3 230.4 %all-to-all-done.2 = f32[32,1,82944]{2,1,0:T(1,128)} async-done(((f32[32,1,82944]{2,1,0:T(1,128)}), f32[32,1,82944]{2,1,0:T(1,128)}, u32[]{:S(2)}, u32[]{:S(2)}) %all-to-all-start.2) | async-done | bytes 10616864 | tf_op jit(solution)/shard_map/all_to_all | solution.py:91
  622.2 102.1 %reduce.2 = f32[32,82944]{1,0:T(8,128)} reduce(f32[32,1,82944]{2,1,0:T(1,128)} %all-to-all-done.2, f32[]{:T(128)} %broadcast.34), dimensions={1}, to_apply=%all_to_all.19.reduce_sub_computation | reduce | bytes 21233668 | tf_op jit(solution)/shard_map/all_to_all | solution.py:91
  724.3 37.8 %reshape.63 = f32[6144,3,144]{2,1,0:T(4,128)} reshape(f32[32,82944]{1,0:T(8,128)} %reduce.2) | data formatting | bytes 21233664
  762.1 22.8 %copy.31 = f32[3,144,32,192]{3,2,1,0:T(8,128)} copy(f32[3,144,32,192]{1,0,3,2:T(4,128)} %bitcast.53) | data formatting | bytes 21233664 | tf_op jit(solution)/shard_map/all_to_all | solution.py:91
  784.9 9.1 fusion
  794.0 278.5 %all-reduce.2 = bf16[8,3,144,192]{3,0,2,1:T(8,128)(2,1)S(1)} all-reduce(f32[8,3,144,192]{3,0,2,1:T(8,128)} %fusion), channel_id=2, replica_groups=mesh['dp'=8,'expert'=32] {'dp'}, use_global_device_ids=true, to_apply=%region_5.6.clone | all-reduce | flops 663552 | bytes 3981312
  1072.5 0.7 dynamic-slice_convert_fusion
  (24 shorter events, 3.3 us)
Async XLA Ops:
  0.0 3.7 copy-start
  12.5 9.4 copy-start.2
  12.5 148.8 %all-to-all-start.1 = ((bf16[32,16,6144]{2,1,0:T(8,128)(2,1)}), bf16[32,16,6144]{2,1,0:T(8,128)(2,1)}, u32[]{:S(2)}, u32[]{:S(2)}) async-start(bf16[32,16,6144]{2,1,0:T(8,128)(2,1)} %copy.25), calls=%async_computation.1 | async-start | bytes 12582912 | tf_op jit(solution)/shard_map/all_to_all | solution.py:77
  30.6 136.8 %copy-start.6 = (s32[32]{0:T(128)S(1)}, s32[32]{0:T(128)}, u32[]{:S(2)}) copy-start(s32[32]{0:T(128)} %param.11) | copy-start | bytes 388
  30.6 137.5 %copy-start.3 = (s32[32,8]{0,1:T(8,128)S(1)}, s32[32,8]{0,1:T(8,128)}, u32[]{:S(2)}) copy-start(s32[32,8]{0,1:T(8,128)} %param.12) | copy-start | bytes 3076
  30.6 137.5 %copy-start.4 = (s32[32]{0:T(128)S(1)}, s32[32]{0:T(128)}, u32[]{:S(2)}) copy-start(s32[32]{0:T(128)} %param.13) | copy-start | bytes 388
  161.3 145.2 %all-to-all-start = ((bf16[32,16,6144]{2,1,0:T(8,128)(2,1)}), bf16[32,16,6144]{2,1,0:T(8,128)(2,1)}, u32[]{:S(2)}, u32[]{:S(2)}) async-start(bf16[32,16,6144]{2,1,0:T(8,128)(2,1)} %copy.21), calls=%async_computation | async-start | bytes 12582912 | tf_op jit(solution)/shard_map/all_to_all | solution.py:80
  383.3 6.4 copy-start.5
  383.3 6.5 copy-start.7
  383.3 238.4 %all-to-all-start.2 = ((f32[32,1,82944]{2,1,0:T(1,128)}), f32[32,1,82944]{2,1,0:T(1,128)}, u32[]{:S(2)}, u32[]{:S(2)}) async-start(f32[32,1,82944]{2,1,0:T(1,128)} %reshape.62), calls=%async_computation.2 | async-start | bytes 21233664 | tf_op jit(solution)/shard_map/all_to_all | solution.py:91
  784.9 288.3 %copy-start.1 = (bf16[8,16,6144]{2,1,0:T(8,128)(2,1)S(1)}, bf16[8,16,6144]{2,1,0:T(8,128)(2,1)}, u32[]{:S(2)}) copy-start(bf16[8,16,6144]{2,1,0:T(8,128)(2,1)} %param.7) | copy-start | bytes 4718596
where the time goes:
time: 1090 us; the launch traced here: 1070 us
  waiting for transfers between devices  484 us (44%)
  blocking collectives  278 us (26%)
  local copies, waits for them, and re-layouts  136 us (12%)
  other arithmetic  110 us (10%)
  matrix products  41.9 us (4%)
  starting transfers between devices  21.9 us (2%)
    unnamed x1, blocking collectives  278 us
    all_to_all x1, waiting for transfers between devices, on_device(): lax.all_to_all(local_grads, 'expert', split_axis=2, concat_axis=0, tiled=...  230 us
    all_to_all x1, waiting for transfers between devices, on_device(): lax.all_to_all(pack_blocks(token_blocks), 'expert', split_axis=0, concat_...  131 us
    all_to_all x1, waiting for transfers between devices, on_device(): lax.all_to_all(pack_blocks(output_grads), 'expert', split_axis=0, concat_...  123 us
    all_to_all x1, other arithmetic, on_device(): lax.all_to_all(local_grads, 'expert', split_axis=2, concat_axis=0, tiled=...  102 us
    unnamed x19, local copies, waits for them, and re-layouts  73.9 us
    all_to_all x2, local copies, waits for them, and re-layouts, on_device(): lax.all_to_all(local_grads, 'expert', split_axis=2, concat_axis=0, tiled=...  23.3 us
    another operation x1, local copies, waits for them, and re-layouts, local_gradients(): return jnp.stack([first, second, third])  22.1 us
  transfers between devices with their start and end apart: 3, of which 3 were waited for; matrix products, arithmetic and copies ran while one was open for 2% of the time, Pallas kernels for 0%

commit v1 on v0

v1 whole, which is shorter than its diff:
```python
import jax
import jax.numpy as jnp
from jax import lax
from jax.experimental import pallas as pl
from jax.experimental.pallas import tpu as pltpu
from jax.sharding import PartitionSpec as P

MESH = pl.DeviceIdType.MESH
EXPERTS = 8
X, Y, Z = 4, 4, 8
GROUP = X * Y
D = 6144
DC = D // GROUP
SLOT = 8
ROWS = 16
MAIN = 128
TAIL = 16
LANES = 512
GROWS = 448
HALF = GROWS // 2
GRAN = Y * ROWS
NGRAN = X * SLOT
TILE = 256
PER_TILE = TILE // GRAN
MAX_TILES = NGRAN // PER_TILE + EXPERTS - 1
VMEM_LIMIT = 56 * 1024 * 1024


def coords():
    d = lax.axis_index("dp")
    c = lax.axis_index("expert")
    return c // 8, d // 2, (d % 2) * 4 + (c // 2) % 4, c % 2


def device(x, y, z, k):
    return (y * 2 + z // 4, (x * 4 + z % 4) * 2 + k)


def plane_peer(x, y, step):
    peer = (x * Y + y + step) % GROUP
    return peer // Y, peer % Y


def signal(sem, target):
    pl.semaphore_signal(sem, inc=1, device_id=target, device_id_type=MESH)


def remote(src, dst, send, recv, target):
    return pltpu.make_async_remote_copy(
        src_ref=src, dst_ref=dst, send_sem=send, recv_sem=recv, device_id=target, device_id_type=MESH
    )


def wait_bytes(ref, sem):
    pltpu.make_async_copy(ref, ref, sem).wait()


def spread_kernel(
    first_col, tok, cot, wts, xg, qg, wg, wr, sel, xs_sem, xr_sem, qs_sem, qr_sem, ws_sem, wr_sem, own_sem,
    rs_sem, rr_sem, ls_sem, lr_sem, ss_sem, sr_sem,
):
    x, y, z, k = coords()
    zh, zl = z // 4, z % 4
    me_col = (x * 4 + zl) * 2 + k
    barrier = pltpu.get_barrier_semaphore()

    def greet_plane(step, carry):
        px, py = plane_peer(x, y, step)
        signal(barrier, device(px, py, z, k))
        return carry

    def greet_column(step, carry):
        signal(barrier, (y * 2 + zh, (me_col + step) % 32))
        return carry

    lax.fori_loop(1, GROUP, greet_plane, 0)
    lax.fori_loop(1, 32, greet_column, 0)
    right, left = device(x, y, (z + 1) % Z, k), device(x, y, (z + Z - 1) % Z, k)
    sibling = device(x, y, z, 1 - k)
    signal(barrier, right)
    signal(barrier, left)
    pl.semaphore_wait(barrier, GROUP - 1 + 31 + 2)

    def weight_piece(col, part):
        cx, cz, ck = col // 8, zh * 4 + (col // 2) % 4, col % 2
        t = jnp.minimum((cz * 2 + ck) * 2 + part, 26)
        tail = t // 24
        m = (t // 8) * (1 - tail) + (t - 24) * tail
        row = (t % 8) * 16 * (1 - tail) + 128 * tail
        return wts.at[
            0,
            m,
            pl.ds(pl.multiple_of(row, 16), 16),
            pl.ds(pl.multiple_of((cx * Y + y) * DC, 128), DC),
        ]

    def send_weights(step, carry):
        col = (me_col + step) % 32
        for part in range(2):
            remote(
                weight_piece(col, part), wr.at[me_col, pl.ds(part * 16, 16), :], ws_sem, wr_sem, (y * 2 + zh, col)
            ).start()
        return carry

    lax.fori_loop(1, 32, send_weights, 0)
    for part in range(2):
        pltpu.make_async_copy(
            weight_piece(me_col, part), wr.at[me_col, pl.ds(part * 16, 16), :], wr_sem
        ).start()

    def columns(ref, px, py):
        return ref.at[:, :, pl.ds(pl.multiple_of((px * Y + py) * DC, 128), DC)]

    def send_rows(step, carry):
        px, py = plane_peer(x, y, step)
        target = device(px, py, z, k)
        remote(columns(tok, px, py), xg.at[x, :, y], xs_sem.at[step], xr_sem.at[step], target).start()
        remote(columns(cot, px, py), qg.at[x, :, y], qs_sem.at[step], qr_sem.at[step], target).start()
        return carry

    lax.fori_loop(1, GROUP, send_rows, 0)
    own_x = pltpu.make_async_copy(columns(tok, x, y), xg.at[x, :, y], own_sem.at[0])
    own_q = pltpu.make_async_copy(columns(cot, x, y), qg.at[x, :, y], own_sem.at[1])
    own_x.start()
    own_q.start()

    wait_bytes(wr, wr_sem)
    for e in range(EXPERTS):
        sel[e] = wr[first_col[e]]

    def chunk(pz):
        return wg.at[:, pl.ds(pl.multiple_of((pz * 2 + k) * 32, 32), 32), :]

    mine = chunk(z)
    own_w = pltpu.make_async_copy(sel, mine, own_sem.at[2])
    own_w.start()
    rights = [remote(sel, mine, rs_sem.at[0], rr_sem.at[0], right)]
    lefts = [remote(sel, mine, ls_sem.at[0], lr_sem.at[0], left)]
    sibs = [remote(sel, mine, ss_sem.at[0], sr_sem.at[0], sibling)]
    rights[0].start()
    lefts[0].start()
    sibs[0].start()
    for t in range(1, 5):
        rights[t - 1].wait_recv()
        piece = chunk((z + Z - t) % Z)
        if t < 4:
            go = remote(piece, piece, rs_sem.at[t], rr_sem.at[t], right)
            go.start()
            rights.append(go)
        go = remote(piece, piece, ss_sem.at[2 * t - 1], sr_sem.at[2 * t - 1], sibling)
        go.start()
        sibs.append(go)
        if t < 4:
            lefts[t - 1].wait_recv()
            piece = chunk((z + t) % Z)
            if t < 3:
                go = remote(piece, piece, ls_sem.at[t], lr_sem.at[t], left)
                go.start()
                lefts.append(go)
            go = remote(piece, piece, ss_sem.at[2 * t], sr_sem.at[2 * t], sibling)
            go.start()
            sibs.append(go)
    for go in sibs:
        go.wait_recv()
    for go in rights + lefts + sibs:
        go.wait_send()
    own_w.wait()
    wait_bytes(wr.at[pl.ds(0, 31)], ws_sem)

    def finish(step, carry):
        px, py = plane_peer(x, y, step)
        target = device(px, py, z, k)
        remote(columns(tok, px, py), xg.at[x, :, y], xs_sem.at[step], xr_sem.at[step], target).wait()
        remote(columns(cot, px, py), qg.at[x, :, y], qs_sem.at[step], qr_sem.at[step], target).wait()
        return carry

    lax.fori_loop(1, GROUP, finish, 0)
    own_x.wait()
    own_q.wait()


def spread(first_col, tok, cot, wts):
    hbm = pl.BlockSpec(memory_space=pl.ANY)
    dma = pltpu.SemaphoreType.DMA
    return pl.pallas_call(
        spread_kernel,
        out_shape=(
            jax.ShapeDtypeStruct((X, SLOT, Y, ROWS, DC), jnp.bfloat16),
            jax.ShapeDtypeStruct((X, SLOT, Y, ROWS, DC), jnp.bfloat16),
            jax.ShapeDtypeStruct((EXPERTS, LANES, DC), jnp.bfloat16),
        ),
        in_specs=[pl.BlockSpec(memory_space=pltpu.SMEM), hbm, hbm, hbm],
        out_specs=(hbm, hbm, hbm),
        scratch_shapes=[
            pltpu.VMEM((32, 32, DC), jnp.bfloat16),
            pltpu.VMEM((EXPERTS, 32, DC), jnp.bfloat16),
            dma((GROUP,)),
            dma((GROUP,)),
            dma((GROUP,)),
            dma((GROUP,)),
            dma,
            dma,
            dma((3,)),
            dma((4,)),
            dma((4,)),
            dma((3,)),
            dma((3,)),
            dma((8,)),
            dma((8,)),
        ],
        compiler_params=pltpu.CompilerParams(
            collective_id=0, has_side_effects=True, vmem_limit_bytes=VMEM_LIMIT
        ),
        name="spread",
    )(first_col, tok, cot, wts)


def place_granules(gexp, pos, owner):
    def clear(t, carry):
        owner[t] = 0
        return carry

    lax.fori_loop(0, MAX_TILES + 1, clear, 0)

    def one_expert(e, tile):
        def one_granule(g, count):
            hit = gexp[g] == e

            @pl.when(hit)
            def _():
                pos[g] = tile * PER_TILE + count

            return count + hit.astype(jnp.int32)

        count = lax.fori_loop(0, NGRAN, one_granule, 0)
        tiles = (count + PER_TILE - 1) // PER_TILE

        def name_tile(t, carry):
            owner[t] = e
            return carry

        lax.fori_loop(tile, tile + tiles, name_tile, 0)
        return tile + tiles

    used = lax.fori_loop(0, EXPERTS, one_expert, 0)

    def dead(g, carry):
        @pl.when(gexp[g] >= EXPERTS)
        def _():
            pos[g] = MAX_TILES * PER_TILE

        return carry

    lax.fori_loop(0, NGRAN, dead, 0)
    return used


def dot_nt(a, b):
    return lax.dot_general(a, b, (((1,), (1,)), ((), ())), preferred_element_type=jnp.float32)


def dot_tn(a, b):
    return lax.dot_general(a, b, (((0,), (0,)), ((), ())), preferred_element_type=jnp.float32)


def sort_rows(pos, pairs):
    for _, packed in pairs:
        packed[...] = jnp.zeros_like(packed)

    def move(g, carry):
        at = pl.ds(pl.multiple_of(pos[g] * GRAN, GRAN), GRAN)
        for source, packed in pairs:
            packed[at] = source[g]
        return carry

    lax.fori_loop(0, NGRAN, move, 0)


def project_kernel(gexp, xg, qg, wg, part, xs, qs, ps, pos, owner):
    used = place_granules(gexp, pos, owner)
    sort_rows(pos, [(xg, xs), (qg, qs)])
    in_tail = lax.broadcasted_iota(jnp.int32, (TILE, MAIN), 1) < 2 * TAIL

    def tile_step(t, carry):
        at = pl.ds(pl.multiple_of(t * TILE, TILE), TILE)
        e = owner[t]
        xt, qt = xs[at], qs[at]
        ps[at, 0 : 2 * MAIN] = dot_nt(xt, wg[e, 0 : 2 * MAIN]).astype(jnp.bfloat16)
        x_tail = dot_nt(xt, wg[e, 3 * MAIN : LANES])
        q_all = dot_nt(qt, wg[e, 2 * MAIN : LANES])
        ps[at, 2 * MAIN : 3 * MAIN] = q_all[:, :MAIN].astype(jnp.bfloat16)
        ps[at, 3 * MAIN : LANES] = jnp.where(in_tail, x_tail, q_all[:, MAIN:]).astype(jnp.bfloat16)
        return carry

    lax.fori_loop(0, used, tile_step, 0)

    def put_back(g, carry):
        rows = ps[pl.ds(pl.multiple_of(pos[g] * GRAN, GRAN), GRAN)]
        for py in range(Y):
            part[g // SLOT, py, g % SLOT] = rows[py * ROWS : (py + 1) * ROWS]
        return carry

    lax.fori_loop(0, NGRAN, put_back, 0)


def project(gexp, xg, qg, wg):
    vmem = pl.BlockSpec(memory_space=pltpu.VMEM)
    packed = (MAX_TILES + 1) * TILE
    return pl.pallas_call(
        project_kernel,
        out_shape=jax.ShapeDtypeStruct((X, Y, SLOT, ROWS, LANES), jnp.bfloat16),
        in_specs=[pl.BlockSpec(memory_space=pltpu.SMEM), vmem, vmem, vmem],
        out_specs=vmem,
        scratch_shapes=[
            pltpu.VMEM((packed, DC), jnp.bfloat16),
            pltpu.VMEM((packed, DC), jnp.bfloat16),
            pltpu.VMEM((packed, LANES), jnp.bfloat16),
            pltpu.SMEM((NGRAN,), jnp.int32),
            pltpu.SMEM((MAX_TILES + 1,), jnp.int32),
        ],
        compiler_params=pltpu.CompilerParams(vmem_limit_bytes=VMEM_LIMIT),
        name="project",
    )(gexp, xg, qg, wg)


def swiglu_rows(gate, up, grad):
    sig = jax.nn.sigmoid(gate)
    act = gate * sig
    return grad * up * sig * (1.0 + gate * (1.0 - sig)), grad * act, act * up


def hidden_kernel(part, hg, got, hid, ps_sem, pr_sem, hs_sem, hr_sem, own_sem):
    x, y, z, k = coords()
    me = x * Y + y
    barrier = pltpu.get_barrier_semaphore()

    def greet(step, carry):
        px, py = plane_peer(x, y, step)
        signal(barrier, device(px, py, z, k))
        return carry

    lax.fori_loop(1, GROUP, greet, 0)
    pl.semaphore_wait(barrier, GROUP - 1)

    def partial_copy(step):
        px, py = plane_peer(x, y, step)
        return remote(
            part.at[px * Y + py], got.at[me], ps_sem.at[step], pr_sem.at[step], device(px, py, z, k)
        )

    def send_partial(step, carry):
        partial_copy(step).start()
        return carry

    lax.fori_loop(1, GROUP, send_partial, 0)
    own = pltpu.make_async_copy(part.at[me], got.at[me], own_sem.at[0])
    own.start()
    own.wait()

    def wait_partial(step, carry):
        partial_copy(step).wait()
        return carry

    lax.fori_loop(1, GROUP, wait_partial, 0)

    lane = lax.broadcasted_iota(jnp.int32, (SLOT * ROWS, MAIN), 1)

    def total(lo):
        out = got[0, :, lo : lo + MAIN].astype(jnp.float32)
        for s in range(1, GROUP):
            out += got[s, :, lo : lo + MAIN].astype(jnp.float32)
        return out

    def shift(v, amount):
        return pltpu.roll(v, amount % MAIN, 1)

    def put(lo, value):
        hid[:, :, lo : lo + MAIN] = value.astype(jnp.bfloat16).reshape(SLOT, ROWS, MAIN)

    for at, value in enumerate(swiglu_rows(total(0), total(MAIN), total(2 * MAIN))):
        put(at * MAIN, value)
    tail = total(3 * MAIN)
    first, second, third = swiglu_rows(tail, shift(tail, -TAIL), shift(tail, -2 * TAIL))
    packed = jnp.where(
        lane < TAIL, first, jnp.where(lane < 2 * TAIL, shift(second, TAIL), shift(third, 2 * TAIL))
    )
    put(3 * MAIN, jnp.where(lane < 3 * TAIL, packed, 0.0))

    def hidden_copy(step):
        px, py = plane_peer(x, y, step)
        return remote(hid, hg.at[x, :, y], hs_sem.at[step], hr_sem.at[step], device(px, py, z, k))

    def send_hidden(step, carry):
        hidden_copy(step).start()
        return carry

    lax.fori_loop(1, GROUP, send_hidden, 0)
    keep = pltpu.make_async_copy(hid, hg.at[x, :, y], own_sem.at[1])
    keep.start()
    keep.wait()

    def wait_hidden(step, carry):
        hidden_copy(step).wait()
        return carry

    lax.fori_loop(1, GROUP, wait_hidden, 0)


def hidden(part):
    hbm = pl.BlockSpec(memory_space=pl.ANY)
    dma = pltpu.SemaphoreType.DMA
    return pl.pallas_call(
        hidden_kernel,
        out_shape=jax.ShapeDtypeStruct((X, SLOT, Y, ROWS, LANES), jnp.bfloat16),
        in_specs=[hbm],
        out_specs=hbm,
        scratch_shapes=[
            pltpu.VMEM((GROUP, SLOT * ROWS, LANES), jnp.bfloat16),
            pltpu.VMEM((SLOT, ROWS, LANES), jnp.bfloat16),
            dma((GROUP,)),
            dma((GROUP,)),
            dma((GROUP,)),
            dma((GROUP,)),
            dma((2,)),
        ],
        compiler_params=pltpu.CompilerParams(
            collective_id=1, has_side_effects=True, vmem_limit_bytes=VMEM_LIMIT
        ),
        name="hidden",
    )(part)


def grads_kernel(gexp, xg, qg, hg, acc, xs, qs, hs, pos, owner):
    used = place_granules(gexp, pos, owner)
    sort_rows(pos, [(xg, xs), (qg, qs), (hg, hs)])
    acc[...] = jnp.zeros_like(acc)
    tail_rows = GROWS - 3 * MAIN
    from_x = lax.broadcasted_iota(jnp.int32, (tail_rows, DC), 0) < 2 * TAIL

    def tile_step(t, carry):
        at = pl.ds(pl.multiple_of(t * TILE, TILE), TILE)
        e = owner[t]
        xt, qt = xs[at], qs[at]
        acc[e, 0 : 2 * MAIN] += dot_tn(hs[at, 0 : 2 * MAIN], xt)
        acc[e, 2 * MAIN : 3 * MAIN] += dot_tn(hs[at, 2 * MAIN : 3 * MAIN], qt)
        tail = hs[at, 3 * MAIN : LANES]
        x_tail, q_tail = dot_tn(tail, xt), dot_tn(tail, qt)
        acc[e, 3 * MAIN : GROWS] += jnp.where(from_x, x_tail[:tail_rows], q_tail[:tail_rows])
        return carry

    lax.fori_loop(0, used, tile_step, 0)


def gradients(gexp, xg, qg, hg):
    vmem = pl.BlockSpec(memory_space=pltpu.VMEM)
    packed = (MAX_TILES + 1) * TILE
    return pl.pallas_call(
        grads_kernel,
        out_shape=jax.ShapeDtypeStruct((EXPERTS, GROWS, DC), jnp.float32),
        in_specs=[pl.BlockSpec(memory_space=pltpu.SMEM), vmem, vmem, vmem],
        out_specs=vmem,
        scratch_shapes=[
            pltpu.VMEM((packed, DC), jnp.bfloat16),
            pltpu.VMEM((packed, DC), jnp.bfloat16),
            pltpu.VMEM((packed, LANES), jnp.bfloat16),
            pltpu.SMEM((NGRAN,), jnp.int32),
            pltpu.SMEM((MAX_TILES + 1,), jnp.int32),
        ],
        compiler_params=pltpu.CompilerParams(vmem_limit_bytes=VMEM_LIMIT),
        name="gradients",
    )(gexp, xg, qg, hg)


def reduce_kernel(grads, out, sib, own, mix, got, send, recv, own_sem, rs_sem, rr_sem):
    x, y, z, k = coords()
    sibling = device(x, y, z, 1 - k)
    barrier = pltpu.get_barrier_semaphore()
    signal(barrier, sibling)

    def greet(step, carry):
        signal(barrier, device(x, y, (z + step) % Z, k))
        return carry

    lax.fori_loop(1, Z, greet, 0)
    pl.semaphore_wait(barrier, Z)

    def half(ref, which):
        return ref.at[:, pl.ds(pl.multiple_of(which * HALF, HALF), HALF), :]

    trade = remote(half(grads, 1 - k), sib, send.at[0], recv.at[0], sibling)
    trade.start()
    keep = pltpu.make_async_copy(half(grads, k), own, own_sem)
    keep.start()
    keep.wait()
    trade.wait()

    def spread_copy(step):
        pz = (z + step) % Z
        return remote(mix.at[pz], got.at[z], rs_sem.at[step], rr_sem.at[step], device(x, y, pz, k))

    def send_sum(step, carry):
        pz = (z + step) % Z
        mix[pz] = (own[pz] + sib[pz]).astype(jnp.bfloat16)
        spread_copy(step).start()
        return carry

    lax.fori_loop(1, Z, send_sum, 0)
    got[z] = (own[z] + sib[z]).astype(jnp.bfloat16)

    def wait_sum(step, carry):
        spread_copy(step).wait()
        return carry

    lax.fori_loop(1, Z, wait_sum, 0)
    value = got[0].astype(jnp.float32)
    for s in range(1, Z):
        value += got[s].astype(jnp.float32)
    mine = out.at[pl.ds(pl.multiple_of(k * HALF, HALF), HALF), :]
    mine[...] = value.astype(jnp.bfloat16)
    swap = remote(mine, mine, send.at[1], recv.at[1], sibling)
    swap.start()
    swap.wait()


def reduce_grads(grads):
    dma = pltpu.SemaphoreType.DMA
    half = pltpu.VMEM((EXPERTS, HALF, DC), jnp.bfloat16)
    wide = pltpu.VMEM((EXPERTS, HALF, DC), jnp.float32)
    return pl.pallas_call(
        reduce_kernel,
        out_shape=jax.ShapeDtypeStruct((GROWS, DC), jnp.bfloat16),
        in_specs=[pl.BlockSpec(memory_space=pl.ANY)],
        out_specs=pl.BlockSpec(memory_space=pltpu.VMEM),
        scratch_shapes=[wide, wide, half, half, dma((2,)), dma((2,)), dma, dma((Z,)), dma((Z,))],
        compiler_params=pltpu.CompilerParams(
            collective_id=2, has_side_effects=True, vmem_limit_bytes=VMEM_LIMIT
        ),
        name="reduce_grads",
    )(grads)


PACK = 96


def deal_kernel(pieces, out, send, recv, own_sem):
    x, y, z, k = coords()
    zh, zl = z // 4, z % 4
    barrier = pltpu.get_barrier_semaphore()

    def target(share):
        return share // 2, (share % 2) * 4 + y

    def source(pz):
        return zl, pz

    def greet_share(share, carry):
        ty, tz = target(share)

        @pl.when((ty != y) | (tz != z))
        def _():
            signal(barrier, device(x, ty, tz, k))

        return carry

    def greet_source(pz, carry):
        @pl.when((zl != y) | (pz != z))
        def _():
            signal(barrier, device(x, zl, pz, k))

        return carry

    lax.fori_loop(0, 8, greet_share, 0)
    lax.fori_loop(0, 8, greet_source, 0)
    self_here = jnp.where(zl == y, 1, 0)
    pl.semaphore_wait(barrier, 16 - 2 * self_here)
    mine = y * 2 + zh

    def start(share, carry):
        ty, tz = target(share)

        @pl.when((ty != y) | (tz != z))
        def _():
            remote(pieces.at[share], out.at[z], send.at[share], recv.at[z], device(x, ty, tz, k)).start()

        @pl.when((ty == y) & (tz == z))
        def _():
            pltpu.make_async_copy(pieces.at[share], out.at[z], own_sem).start()

        return carry

    def finish_send(share, carry):
        ty, tz = target(share)

        @pl.when((ty != y) | (tz != z))
        def _():
            remote(
                pieces.at[share], out.at[z], send.at[share], recv.at[z], device(x, ty, tz, k)
            ).wait_send()

        @pl.when((ty == y) & (tz == z))
        def _():
            pltpu.make_async_copy(pieces.at[share], out.at[z], own_sem).wait()

        return carry

    def finish_recv(pz, carry):
        @pl.when((zl != y) | (pz != z))
        def _():
            pltpu.make_async_copy(out.at[pz], out.at[pz], recv.at[pz]).wait()

        return carry

    lax.fori_loop(0, 8, start, 0)
    lax.fori_loop(0, 8, finish_send, 0)
    lax.fori_loop(0, 8, finish_recv, 0)


def deal(pieces):
    dma = pltpu.SemaphoreType.DMA
    vmem = pl.BlockSpec(memory_space=pltpu.VMEM)
    return pl.pallas_call(
        deal_kernel,
        out_shape=jax.ShapeDtypeStruct((EXPERTS, PACK, 128), jnp.bfloat16),
        in_specs=[vmem],
        out_specs=vmem,
        scratch_shapes=[dma((8,)), dma((8,)), dma],
        compiler_params=pltpu.CompilerParams(
            collective_id=3, has_side_effects=True, vmem_limit_bytes=VMEM_LIMIT
        ),
        name="deal",
    )(pieces)


def on_device(tok, cot, wts, counts, column, dest, live):
    c = lax.axis_index("expert")
    in_plane = c % 8
    ids = jnp.arange(EXPERTS, dtype=jnp.int32)
    cumulative = jnp.sum(jnp.where(ids[None, :] <= ids[:, None], counts[None, :], 0), axis=1)
    first = cumulative - counts
    replicas = jnp.arange(32, dtype=jnp.int32)
    first_col = jnp.sum(jnp.where(replicas[None, :] == first[:, None], column[None, :], 0), axis=1)
    my_dest = lax.dynamic_index_in_dim(dest.reshape(X, 8, SLOT), in_plane, 1, keepdims=False)
    my_live = lax.dynamic_index_in_dim(live.reshape(X, 8), in_plane, 1, keepdims=False)
    expert = jnp.sum((cumulative[None, None, :] <= my_dest[:, :, None]).astype(jnp.int32), axis=2)
    slots = jnp.arange(SLOT, dtype=jnp.int32)
    gexp = jnp.where(slots[None, :] < my_live[:, None], expert, EXPERTS).reshape(NGRAN)

    xg, qg, wg = spread(first_col, tok, cot, wts)
    xg = xg.reshape(NGRAN, GRAN, DC)
    qg = qg.reshape(NGRAN, GRAN, DC)
    part = project(gexp, xg, qg, wg)
    hg = hidden(part.reshape(GROUP, SLOT * ROWS, LANES)).reshape(NGRAN, GRAN, LANES)
    grads = reduce_grads(gradients(gexp, xg, qg, hg))

    main = grads[: 3 * MAIN].reshape(3, MAIN, DC)
    rest = grads[3 * MAIN : 3 * MAIN + 3 * TAIL].reshape(3, TAIL, DC)
    whole = jnp.concatenate([main, rest], axis=1)
    ours = lax.dynamic_slice_in_dim(whole, (c % 2) * (DC // 2), DC // 2, 2)
    shares = ours.reshape(3, 8, 18, DC // 2).transpose(1, 0, 2, 3).reshape(8, 81, 128)
    pieces = jnp.pad(shares, ((0, 0), (0, PACK - 81), (0, 0)))
    return deal(pieces)[:, :81].reshape(EXPERTS, 3, 18, DC // 2)


def solution(mesh):
    placed = (
        P("expert", "dp", None),
        P("expert", "dp", None),
        P("expert", None, None, None),
        P(),
        P(),
        P(),
        P(),
    )
    return jax.shard_map(
        on_device,
        mesh=mesh,
        in_specs=placed,
        out_specs=P(None, None, "dp", "expert"),
        check_vma=False,
    )
```

time: 1090 us -> 251 us (0.23); the launches traced: 1070 us -> 249 us
  waiting for transfers between devices: 484 us -> 0 us
  blocking collectives: 278 us -> 0 us
  Pallas kernels: 0 us -> 238 us
  local copies, waits for them, and re-layouts: 136 us -> 7.3 us
  other arithmetic: 110 us -> 3.2 us
  matrix products: 41.9 us -> 0 us
  starting transfers between devices: 21.9 us -> 0 us
    all_to_all x3 -> x0, waiting for transfers between devices: 484 us -> none  [the longest x1 230 us: on_device(): lax.all_to_all(local_grads, 'expert', split_axis=2, concat_axis=0, tiled=...]
    unnamed x1 -> x0, blocking collectives: 278 us -> none
    pallas_call x0 -> x6, Pallas kernels: none -> 238 us  [the longest x1 78.8 us: hidden(): pl.pallas_call(hidden_kernel, out_shape=jax.ShapeDtypeStruct((X, SLOT, Y,...]
    all_to_all x1 -> x0, other arithmetic: 102 us -> none  [on_device(): lax.all_to_all(local_grads, 'expert', split_axis=2, concat_axis=0, tiled=...]
    unnamed x19 -> x1, local copies, waits for them, and re-layouts: 73.9 us -> 0.11 us
    dot_general x11 -> x0, matrix products: 41.9 us -> none  [the longest x2 19.2 us: unpack_blocks(): jnp.einsum('sj,jrd->srd', receive_pick, received, preferred_element_type=...]
    all_to_all x2 -> x0, local copies, waits for them, and re-layouts: 23.3 us -> none  [on_device(): lax.all_to_all(local_grads, 'expert', split_axis=2, concat_axis=0, tiled=...]
    another operation x1 -> x0, local copies, waits for them, and re-layouts: 22.1 us -> none  [local_gradients(): return jnp.stack([first, second, third])]
  transfers between devices with their start and end apart: 3 -> 0, of which waited for: 3 -> 0; matrix products, arithmetic and copies ran while one was open for 2% -> 0% of each run, Pallas kernels for 0% -> 0%
where the time goes in v1:
time: 251 us; the launch traced here: 249 us
  Pallas kernels  238 us (95%)
  local copies, waits for them, and re-layouts  7.3 us (3%)
  other arithmetic  3.2 us (1%)
    pallas_call x1, Pallas kernels, hidden(): pl.pallas_call(hidden_kernel, out_shape=jax.ShapeDtypeStruct((X, SLOT, Y,...  78.8 us
    pallas_call x1, Pallas kernels, spread(): pl.pallas_call(spread_kernel, out_shape=(jax.ShapeDtypeStruct((X, SLOT, Y...  74.9 us
    pallas_call x1, Pallas kernels, reduce_grads(): pl.pallas_call(reduce_kernel, out_shape=jax.ShapeDtypeStruct((GROWS, DC),...  43.3 us
    pallas_call x1, Pallas kernels, deal(): pl.pallas_call(deal_kernel, out_shape=jax.ShapeDtypeStruct((EXPERTS, PACK...  17.4 us
    pallas_call x1, Pallas kernels, gradients(): pl.pallas_call(grads_kernel, out_shape=jax.ShapeDtypeStruct((EXPERTS, GRO...  12.6 us
    pallas_call x1, Pallas kernels, project(): pl.pallas_call(project_kernel, out_shape=jax.ShapeDtypeStruct((X, Y, SLOT...  11.5 us

profile of v1, /device:TPU:25, one launch (start us, length us, event | category | flops | bytes accessed | tf_op | source)
XLA Modules:
  0.0 249.1 jit_solution(11873766700548608131)
XLA Ops:
  0.0 0.8 select_reduce_fusion.1
  0.8 0.7 sub.3
  1.4 1.3 select_reduce_fusion.first_col
  2.7 0.7 reshape.46
  3.5 0.2 dynamic-slice_reduce_fusion
  3.7 0.8 reshape.47
  4.4 0.1 constant_dynamic-slice_fusion
  4.5 0.1 copy.16
  4.6 0.2 convert_reduce_fusion
  4.8 0.1 fusion.1
  4.9 0.6 select_n.40.gexp
  5.5 74.9 %spread.1 = (bf16[4,8,4,16,384]{4,3,2,1,0:T(8,128)(2,1)}, bf16[4,8,4,16,384]{4,3,2,1,0:T(8,128)(2,1)}, bf16[8,512,384]{2,1,0:T(8,128)(2,1)}) custom-call(s32[8]{0:T(128)} %select_reduce_fusion.first_col, bf16[8,16,6144]{2,1,0:T(8,128)(2,1)} %tok.1, bf16[8,16,6144]{2,1,0:T(8,128)(2,1)} %cot.1, bf16[1,3,144,6144]{3,2,1,0:T(8,128)(2,1)} %wts.1), custom_call_target="tpu_custom_call" | custom-call | tf_op jit(solution)/shard_map/spread/pallas_call | solution.py:185
  80.5 11.5 %project.1 = bf16[4,4,8,16,512]{4,3,2,1,0:T(8,128)(2,1)} custom-call(s32[32]{0:T(128)} %select_n.40.gexp, bf16[32,64,384]{2,1,0:T(8,128)(2,1)} %bitcast.12, bf16[32,64,384]{2,1,0:T(8,128)(2,1)} %bitcast.14, bf16[8,512,384]{2,1,0:T(8,128)(2,1)} %get-tuple-element.10.wg), custom_call_target="tpu_custom_call" | custom-call | tf_op jit(solution)/shard_map/project/pallas_call | solution.py:309
  92.0 78.8 %hidden.1 = bf16[4,8,4,16,512]{4,3,2,1,0:T(8,128)(2,1)} custom-call(bf16[16,128,512]{2,1,0:T(8,128)(2,1)} %bitcast.11), custom_call_target="tpu_custom_call" | custom-call | tf_op jit(solution)/shard_map/hidden/pallas_call | solution.py:412
  170.8 12.6 %gradients.1.grads = f32[8,448,384]{2,1,0:T(8,128)} custom-call(s32[32]{0:T(128)} %select_n.40.gexp, bf16[32,64,384]{2,1,0:T(8,128)(2,1)} %bitcast.13, bf16[32,64,384]{2,1,0:T(8,128)(2,1)} %bitcast.15, bf16[32,64,512]{2,1,0:T(8,128)(2,1)} %bitcast.10), custom_call_target="tpu_custom_call" | custom-call | tf_op jit(solution)/shard_map/gradients/pallas_call | solution.py:457
  183.3 43.3 %reduce_grads.1 = bf16[448,384]{1,0:T(8,128)(2,1)} custom-call(f32[8,448,384]{2,1,0:T(8,128)} %gradients.1.grads), custom_call_target="tpu_custom_call" | custom-call | tf_op jit(solution)/shard_map/reduce_grads/pallas_call | solution.py:529
  226.6 0.8 slice.10
  227.4 1.0 slice.9
  228.4 0.2 fusion
  228.6 0.1 reshape.54
  228.7 0.3 reshape.55
  229.0 0.7 pad.4.pieces
  229.7 17.4 %deal.1 = bf16[8,96,128]{2,1,0:T(8,128)(2,1)} custom-call(bf16[8,96,128]{2,1,0:T(8,128)(2,1)} %pad.4.pieces), custom_call_target="tpu_custom_call" | custom-call | tf_op jit(solution)/shard_map/deal/pallas_call | solution.py:621
  247.1 0.9 slice.11
  248.1 0.3 reshape.56
  248.3 0.7 copy.15
  (1 shorter events, 0.0 us)

commit v2 on v1

v2 whole, which is shorter than its diff:
```python
import jax
import jax.numpy as jnp
from jax import lax
from jax.experimental import pallas as pl
from jax.experimental.pallas import tpu as pltpu
from jax.sharding import PartitionSpec as P

MESH = pl.DeviceIdType.MESH
EXPERTS = 8
X, Y, Z = 4, 4, 8
GROUP = X * Y
D = 6144
DC = D // GROUP
SLOT = 8
ROWS = 16
MAIN = 128
TAIL = 16
LANES = 512
GROWS = 448
HALF = GROWS // 2
GRAN = Y * ROWS
NGRAN = X * SLOT
TILE = 256
PER_TILE = TILE // GRAN
MAX_TILES = NGRAN // PER_TILE + EXPERTS - 1
VMEM_LIMIT = 56 * 1024 * 1024


def coords():
    d = lax.axis_index("dp")
    c = lax.axis_index("expert")
    return c // 8, d // 2, (d % 2) * 4 + (c // 2) % 4, c % 2


def device(x, y, z, k):
    return (y * 2 + z // 4, (x * 4 + z % 4) * 2 + k)


def plane_peer(x, y, step):
    peer = (x * Y + y + step) % GROUP
    return peer // Y, peer % Y


def signal(sem, target):
    pl.semaphore_signal(sem, inc=1, device_id=target, device_id_type=MESH)


def remote(src, dst, send, recv, target):
    return pltpu.make_async_remote_copy(
        src_ref=src, dst_ref=dst, send_sem=send, recv_sem=recv, device_id=target, device_id_type=MESH
    )


def wait_bytes(ref, sem):
    pltpu.make_async_copy(ref, ref, sem).wait()


def swiglu_rows(gate, up, grad):
    sig = jax.nn.sigmoid(gate)
    act = gate * sig
    return grad * up * sig * (1.0 + gate * (1.0 - sig)), grad * act, act * up


def place_granules(gexp, pos, owner, packed):
    def one_expert(e, tile):
        def one_granule(g, count):
            hit = gexp[g] == e

            @pl.when(hit)
            def _():
                pos[g] = tile * PER_TILE + count

            return count + hit.astype(jnp.int32)

        count = lax.fori_loop(0, NGRAN, one_granule, 0)
        tiles = (count + PER_TILE - 1) // PER_TILE

        def name_tile(t, carry):
            owner[t] = e
            return carry

        lax.fori_loop(tile, tile + tiles, name_tile, 0)

        def pad(g, carry):
            at = pl.ds(pl.multiple_of(g * GRAN, GRAN), GRAN)
            for ref in packed:
                ref[at] = jnp.zeros((GRAN, ref.shape[1]), ref.dtype)
            return carry

        lax.fori_loop(tile * PER_TILE + count, (tile + tiles) * PER_TILE, pad, 0)
        return tile + tiles

    used = lax.fori_loop(0, EXPERTS, one_expert, 0)

    def dead(g, carry):
        @pl.when(gexp[g] >= EXPERTS)
        def _():
            pos[g] = MAX_TILES * PER_TILE

        return carry

    lax.fori_loop(0, NGRAN, dead, 0)
    return used


def dot_nt(a, b):
    return lax.dot_general(a, b, (((1,), (1,)), ((), ())), preferred_element_type=jnp.float32)


def dot_tn(a, b):
    return lax.dot_general(a, b, (((0,), (0,)), ((), ())), preferred_element_type=jnp.float32)


def sort_rows(pos, pairs):
    def move(g, carry):
        at = pl.ds(pl.multiple_of(pos[g] * GRAN, GRAN), GRAN)
        for source, packed in pairs:
            packed[at] = source[g]
        return carry

    lax.fori_loop(0, NGRAN, move, 0)


CHUNKS = 2
PART = SLOT // CHUNKS
SUM_TYPE = jnp.float32


def rows_kernel(
    first_col, gexp, tok, cot, wts, xg, qg, hg, wr, sel, wg, xv, qv, p1, r1, s2, r2, hid, xs_sem, xr_sem, qs_sem, qr_sem,
    ws_sem, wr_sem, own_sem, rs_sem, rr_sem, ls_sem, lr_sem, ss_sem, sr_sem, p1s_sem, p1r_sem, p2s_sem, p2r_sem,
    has_sem, har_sem, hbs_sem, hbr_sem, keep_sem,
):
    x, y, z, k = coords()
    zh, zl = z // 4, z % 4
    me_col = (x * 4 + zl) * 2 + k
    barrier = pltpu.get_barrier_semaphore()

    def greet_plane(step, carry):
        px, py = plane_peer(x, y, step)
        signal(barrier, device(px, py, z, k))
        return carry

    def greet_column(step, carry):
        signal(barrier, (y * 2 + zh, (me_col + step) % 32))
        return carry

    lax.fori_loop(1, GROUP, greet_plane, 0)
    lax.fori_loop(1, 32, greet_column, 0)
    right, left = device(x, y, (z + 1) % Z, k), device(x, y, (z + Z - 1) % Z, k)
    sibling = device(x, y, z, 1 - k)
    signal(barrier, right)
    signal(barrier, left)
    pl.semaphore_wait(barrier, GROUP - 1 + 31 + 2)

    def weight_piece(col, part):
        cx, cz, ck = col // 8, zh * 4 + (col // 2) % 4, col % 2
        t = jnp.minimum((cz * 2 + ck) * 2 + part, 26)
        tail = t // 24
        m = (t // 8) * (1 - tail) + (t - 24) * tail
        row = (t % 8) * 16 * (1 - tail) + 128 * tail
        return wts.at[
            0,
            m,
            pl.ds(pl.multiple_of(row, 16), 16),
            pl.ds(pl.multiple_of((cx * Y + y) * DC, 128), DC),
        ]

    def send_weights(step, carry):
        col = (me_col + step) % 32
        for part in range(2):
            remote(
                weight_piece(col, part), wr.at[me_col, pl.ds(part * 16, 16), :], ws_sem, wr_sem, (y * 2 + zh, col)
            ).start()
        return carry

    lax.fori_loop(1, 32, send_weights, 0)
    for part in range(2):
        pltpu.make_async_copy(
            weight_piece(me_col, part), wr.at[me_col, pl.ds(part * 16, 16), :], wr_sem
        ).start()

    def columns(ref, px, py):
        return ref.at[:, :, pl.ds(pl.multiple_of((px * Y + py) * DC, 128), DC)]

    def x_copy(step):
        px, py = plane_peer(x, y, step)
        return remote(
            columns(tok, px, py), xv.at[x, :, y], xs_sem.at[step], xr_sem.at[step], device(px, py, z, k)
        )

    def q_copy(step):
        px, py = plane_peer(x, y, step)
        return remote(
            columns(cot, px, py), qv.at[x, :, y], qs_sem.at[step], qr_sem.at[step], device(px, py, z, k)
        )

    def start_x(step, carry):
        x_copy(step).start()
        return carry

    def start_q(step, carry):
        q_copy(step).start()
        return carry

    lax.fori_loop(1, GROUP, start_x, 0)
    own_x = pltpu.make_async_copy(columns(tok, x, y), xv.at[x, :, y], own_sem.at[0])
    own_q = pltpu.make_async_copy(columns(cot, x, y), qv.at[x, :, y], own_sem.at[1])
    own_x.start()
    own_q.start()

    wait_bytes(wr, wr_sem)
    for e in range(EXPERTS):
        sel[e] = wr[first_col[e]]

    def chunk(pz):
        return wg.at[:, pl.ds(pl.multiple_of((pz * 2 + k) * 32, 32), 32), :]

    mine = chunk(z)
    own_w = pltpu.make_async_copy(sel, mine, own_sem.at[2])
    own_w.start()
    rights = [remote(sel, mine, rs_sem.at[0], rr_sem.at[0], right)]
    lefts = [remote(sel, mine, ls_sem.at[0], lr_sem.at[0], left)]
    sibs = [remote(sel, mine, ss_sem.at[0], sr_sem.at[0], sibling)]
    rights[0].start()
    lefts[0].start()
    sibs[0].start()
    lax.fori_loop(1, GROUP, start_q, 0)
    for t in range(1, 5):
        rights[t - 1].wait_recv()
        piece = chunk((z + Z - t) % Z)
        if t < 4:
            go = remote(piece, piece, rs_sem.at[t], rr_sem.at[t], right)
            go.start()
            rights.append(go)
        go = remote(piece, piece, ss_sem.at[2 * t - 1], sr_sem.at[2 * t - 1], sibling)
        go.start()
        sibs.append(go)
        if t < 4:
            lefts[t - 1].wait_recv()
            piece = chunk((z + t) % Z)
            if t < 3:
                go = remote(piece, piece, ls_sem.at[t], lr_sem.at[t], left)
                go.start()
                lefts.append(go)
            go = remote(piece, piece, ss_sem.at[2 * t], sr_sem.at[2 * t], sibling)
            go.start()
            sibs.append(go)
    for go in sibs:
        go.wait_recv()
    own_w.wait()

    def wait_rows(step, carry):
        x_copy(step).wait()
        q_copy(step).wait()
        return carry

    lax.fori_loop(1, GROUP, wait_rows, 0)
    own_x.wait()
    own_q.wait()
    keep_x = pltpu.make_async_copy(xv, xg, keep_sem.at[0])
    keep_q = pltpu.make_async_copy(qv, qg, keep_sem.at[1])
    keep_x.start()
    keep_q.start()

    a_here, b_here = x * (1 - k) + y * k, x * k + y * (1 - k)

    def place(a, b):
        return a * (1 - k) + b * k, a * k + b * (1 - k)

    def plane_device(a, b):
        px, py = place(a, b)
        return device(px, py, z, k)

    def slots(h):
        return pl.ds(h * PART, PART)

    in_tail = lax.broadcasted_iota(jnp.int32, (GRAN, MAIN), 1) < 2 * TAIL

    def first_copy(h, j):
        a = (a_here + j) % 4
        at = h * 3 + j - 1
        return remote(
            p1.at[a, :, slots(h)], r1.at[a_here, :, slots(h)], p1s_sem.at[at], p1r_sem.at[at], plane_device(a, b_here)
        )

    def second_copy(h, j):
        b = (b_here + j) % 4
        at = h * 3 + j - 1
        return remote(
            s2.at[b, slots(h)], r2.at[b_here, slots(h)], p2s_sem.at[at], p2r_sem.at[at], plane_device(a_here, b)
        )

    def hidden_place(a, b, h):
        px, py = place(a, b)
        return hg.at[px, slots(h), py]

    def hidden_first(h, j):
        at = h * 3 + j - 1
        return remote(
            hid.at[slots(h)], hidden_place(a_here, b_here, h), has_sem.at[at], har_sem.at[at],
            plane_device((a_here + j) % 4, b_here),
        )

    def hidden_second(h, j, i):
        at = (h * 4 + j) * 3 + i - 1
        here = hidden_place((a_here + 4 - j) % 4, b_here, h)
        return remote(
            hid.at[slots(h)] if j == 0 else here, here, hbs_sem.at[at], hbr_sem.at[at],
            plane_device(a_here, (b_here + i) % 4),
        )

    for h in range(CHUNKS):

        def granule(i, carry):
            px, s = i // PART, h * PART + i % PART
            e = jnp.minimum(gexp[px * SLOT + s], EXPERTS - 1)
            xt = xv[px, s].reshape(GRAN, DC)
            qt = qv[px, s].reshape(GRAN, DC)
            x_main = dot_nt(xt, wg[e, 0 : 2 * MAIN]).astype(SUM_TYPE)
            x_tail = dot_nt(xt, wg[e, 3 * MAIN : LANES])
            q_all = dot_nt(qt, wg[e, 2 * MAIN : LANES])
            q_main = q_all[:, :MAIN].astype(SUM_TYPE)
            tail = jnp.where(in_tail, x_tail, q_all[:, MAIN:]).astype(SUM_TYPE)
            for py in range(Y):
                pa, pb = px * (1 - k) + py * k, px * k + py * (1 - k)
                cut = slice(py * ROWS, (py + 1) * ROWS)
                p1[pa, pb, s, :, 0 : 2 * MAIN] = x_main[cut]
                p1[pa, pb, s, :, 2 * MAIN : 3 * MAIN] = q_main[cut]
                p1[pa, pb, s, :, 3 * MAIN : LANES] = tail[cut]
            return carry

        lax.fori_loop(0, X * PART, granule, 0)
        for j in (2, 1, 3):
            first_copy(h, j).start()

    for h in range(CHUNKS):
        for j in (1, 2, 3):
            first_copy(h, j).wait_recv()

        def sum_first(b, carry):
            value = p1[a_here, b, h * PART : (h + 1) * PART].astype(jnp.float32)
            for j in (1, 2, 3):
                value += r1[(a_here + j) % 4, b, h * PART : (h + 1) * PART].astype(jnp.float32)
            s2[b, h * PART : (h + 1) * PART] = value
            return carry

        lax.fori_loop(0, 4, sum_first, 0)
        for j in (2, 1, 3):
            second_copy(h, j).start()

    lane = lax.broadcasted_iota(jnp.int32, (PART * ROWS, MAIN), 1)

    def shift(v, amount):
        return pltpu.roll(v, amount % MAIN, 1)

    for h in range(CHUNKS):
        for j in (1, 2, 3):
            second_copy(h, j).wait_recv()
        cut = slice(h * PART, (h + 1) * PART)

        def total(lo):
            value = s2[b_here, cut, :, lo : lo + MAIN]
            for j in (1, 2, 3):
                value += r2[(b_here + j) % 4, cut, :, lo : lo + MAIN]
            return value.reshape(PART * ROWS, MAIN)

        def put(lo, value):
            hid[cut, :, lo : lo + MAIN] = value.astype(jnp.bfloat16).reshape(PART, ROWS, MAIN)

        for at, value in enumerate(swiglu_rows(total(0), total(MAIN), total(2 * MAIN))):
            put(at * MAIN, value)
        tail = total(3 * MAIN)
        first, second, third = swiglu_rows(tail, shift(tail, -TAIL), shift(tail, -2 * TAIL))
        packed = jnp.where(
            lane < TAIL, first, jnp.where(lane < 2 * TAIL, shift(second, TAIL), shift(third, 2 * TAIL))
        )
        put(3 * MAIN, jnp.where(lane < 3 * TAIL, packed, 0.0))
        for j in (2, 1, 3):
            hidden_first(h, j).start()
        for i in (2, 1, 3):
            hidden_second(h, 0, i).start()
        pltpu.make_async_copy(hid.at[slots(h)], hidden_place(a_here, b_here, h), keep_sem.at[2 + h]).start()

    for h in range(CHUNKS):
        for j in (1, 3, 2):
            hidden_first(h, j).wait_recv()
            for i in (2, 1, 3):
                hidden_second(h, j, i).start()
    for h in range(CHUNKS):
        for j in range(4):
            for i in (1, 2, 3):
                hidden_second(h, j, i).wait()
        for j in (1, 2, 3):
            hidden_first(h, j).wait_send()
            first_copy(h, j).wait_send()
            second_copy(h, j).wait_send()
        pltpu.make_async_copy(hid.at[slots(h)], hidden_place(a_here, b_here, h), keep_sem.at[2 + h]).wait()
    for go in rights + lefts + sibs:
        go.wait_send()
    wait_bytes(wr.at[pl.ds(0, 31)], ws_sem)
    keep_x.wait()
    keep_q.wait()


def rows_and_hidden(first_col, gexp, tok, cot, wts):
    hbm = pl.BlockSpec(memory_space=pl.ANY)
    smem = pl.BlockSpec(memory_space=pltpu.SMEM)
    dma = pltpu.SemaphoreType.DMA
    spread = pltpu.VMEM((X, SLOT, Y, ROWS, DC), jnp.bfloat16)
    sums = pltpu.VMEM((4, 4, SLOT, ROWS, LANES), SUM_TYPE)
    halfway = pltpu.VMEM((4, SLOT, ROWS, LANES), jnp.float32)
    return pl.pallas_call(
        rows_kernel,
        out_shape=(
            jax.ShapeDtypeStruct((X, SLOT, Y, ROWS, DC), jnp.bfloat16),
            jax.ShapeDtypeStruct((X, SLOT, Y, ROWS, DC), jnp.bfloat16),
            jax.ShapeDtypeStruct((X, SLOT, Y, ROWS, LANES), jnp.bfloat16),
        ),
        in_specs=[smem, smem, hbm, hbm, hbm],
        out_specs=(hbm, hbm, hbm),
        scratch_shapes=[
            pltpu.VMEM((32, 32, DC), jnp.bfloat16),
            pltpu.VMEM((EXPERTS, 32, DC), jnp.bfloat16),
            pltpu.VMEM((EXPERTS, LANES, DC), jnp.bfloat16),
            spread,
            spread,
            sums,
            sums,
            halfway,
            halfway,
            pltpu.VMEM((SLOT, ROWS, LANES), jnp.bfloat16),
            dma((GROUP,)),
            dma((GROUP,)),
            dma((GROUP,)),
            dma((GROUP,)),
            dma,
            dma,
            dma((3,)),
            dma((4,)),
            dma((4,)),
            dma((3,)),
            dma((3,)),
            dma((8,)),
            dma((8,)),
            dma((3 * CHUNKS,)),
            dma((3 * CHUNKS,)),
            dma((3 * CHUNKS,)),
            dma((3 * CHUNKS,)),
            dma((3 * CHUNKS,)),
            dma((3 * CHUNKS,)),
            dma((12 * CHUNKS,)),
            dma((12 * CHUNKS,)),
            dma((2 + CHUNKS,)),
        ],
        compiler_params=pltpu.CompilerParams(
            collective_id=0, has_side_effects=True, vmem_limit_bytes=VMEM_LIMIT
        ),
        name="rows_and_hidden",
    )(first_col, gexp, tok, cot, wts)


def grads_kernel(gexp, xg, qg, hg, acc, xs, qs, hs, pos, owner):
    used = place_granules(gexp, pos, owner, [xs, qs, hs])
    sort_rows(pos, [(xg, xs), (qg, qs), (hg, hs)])
    acc[...] = jnp.zeros_like(acc)
    tail_rows = GROWS - 3 * MAIN
    from_x = lax.broadcasted_iota(jnp.int32, (tail_rows, DC), 0) < 2 * TAIL

    def tile_step(t, carry):
        at = pl.ds(pl.multiple_of(t * TILE, TILE), TILE)
        e = owner[t]
        xt, qt = xs[at], qs[at]
        acc[e, 0 : 2 * MAIN] += dot_tn(hs[at, 0 : 2 * MAIN], xt)
        acc[e, 2 * MAIN : 3 * MAIN] += dot_tn(hs[at, 2 * MAIN : 3 * MAIN], qt)
        tail = hs[at, 3 * MAIN : LANES]
        x_tail, q_tail = dot_tn(tail, xt), dot_tn(tail, qt)
        acc[e, 3 * MAIN : GROWS] += jnp.where(from_x, x_tail[:tail_rows], q_tail[:tail_rows])
        return carry

    lax.fori_loop(0, used, tile_step, 0)


def gradients(gexp, xg, qg, hg):
    vmem = pl.BlockSpec(memory_space=pltpu.VMEM)
    packed = (MAX_TILES + 1) * TILE
    return pl.pallas_call(
        grads_kernel,
        out_shape=jax.ShapeDtypeStruct((EXPERTS, GROWS, DC), jnp.float32),
        in_specs=[pl.BlockSpec(memory_space=pltpu.SMEM), vmem, vmem, vmem],
        out_specs=vmem,
        scratch_shapes=[
            pltpu.VMEM((packed, DC), jnp.bfloat16),
            pltpu.VMEM((packed, DC), jnp.bfloat16),
            pltpu.VMEM((packed, LANES), jnp.bfloat16),
            pltpu.SMEM((NGRAN,), jnp.int32),
            pltpu.SMEM((MAX_TILES + 1,), jnp.int32),
        ],
        compiler_params=pltpu.CompilerParams(vmem_limit_bytes=VMEM_LIMIT),
        name="gradients",
    )(gexp, xg, qg, hg)


QUART = HALF // 2
PACK = 64
WINDOW = 256
OFFSETS = (4, 3, -3, 2, -2, 1, -1, 0)


def reduce_kernel(
    grads, out, own, sib, sbuf, rbuf, fin, win, wide, pack, os_sem, ts_sem, tr_sem, cs_sem, cr_sem, swap_sem, send, recv,
    keep_sem,
):
    x, y, z, k = coords()
    zh, zl = z // 4, z % 4
    sibling = device(x, y, z, 1 - k)
    barrier = pltpu.get_barrier_semaphore()

    def target(share):
        return share // 2, (share % 2) * 4 + y

    def greet_share(share, carry):
        ty, tz = target(share)

        @pl.when((ty != y) | (tz != z))
        def _():
            signal(barrier, device(x, ty, tz, k))

        return carry

    def greet_source(pz, carry):
        @pl.when((zl != y) | (pz != z))
        def _():
            signal(barrier, device(x, zl, pz, k))

        return carry

    ahead = (device(x, y, (z + 1) % Z, k), device(x, y, (z + Z - 1) % Z, k))
    signal(barrier, sibling)
    signal(barrier, ahead[0])
    signal(barrier, ahead[1])
    lax.fori_loop(0, 8, greet_share, 0)
    lax.fori_loop(0, 8, greet_source, 0)
    self_here = jnp.where(zl == y, 1, 0)
    pl.semaphore_wait(barrier, 19 - 2 * self_here)

    def half(e, which):
        return grads.at[e, pl.ds(pl.multiple_of(which * HALF, HALF), HALF), :]

    trades, keeps = {}, {}
    for i, off in enumerate(OFFSETS):
        e = (z + off + Z) % Z
        trades[off] = remote(half(e, 1 - k), sib.at[e], ts_sem.at[i], tr_sem.at[i], sibling)
        keeps[off] = pltpu.make_async_copy(half(e, k), own.at[e], os_sem.at[i])
        trades[off].start()
        keeps[off].start()
    trades[-4], keeps[-4] = trades[4], keeps[4]
    ready = set()

    def ours(off, j):
        if abs(off) % 8 == 4:
            off = 4
        if off not in ready:
            trades[off].wait_recv()
            keeps[off].wait()
            ready.add(off)
        e = (z + off + Z) % Z
        cut = slice(j * QUART, (j + 1) * QUART)
        return own[e, cut] + sib[e, cut]

    chain = {}
    for dist in (4, 3, 2, 1):
        for way in range(2):
            for j in range(2):
                longest = 4 if way == j else 3
                if dist > longest:
                    continue
                value = ours(dist if way == 0 else -dist, j)
                if dist < longest:
                    chain[way, j, dist + 1].wait_recv()
                    value += rbuf[way, j, dist].astype(jnp.float32)
                sbuf[way, j, dist - 1] = value.astype(jnp.bfloat16)
                at = (way * 2 + j) * 4 + dist - 1
                go = remote(
                    sbuf.at[way, j, dist - 1], rbuf.at[way, j, dist - 1], cs_sem.at[at], cr_sem.at[at], ahead[way]
                )
                go.start()
                chain[way, j, dist] = go
    for j in range(2):
        value = ours(0, j)
        for way in range(2):
            chain[way, j, 1].wait_recv()
            value += rbuf[way, j, 0].astype(jnp.float32)
        fin[pl.ds(pl.multiple_of(k * HALF + j * QUART, 16), QUART)] = value
    mine = fin.at[pl.ds(pl.multiple_of(k * HALF, HALF), HALF)]
    swap = remote(mine, mine, swap_sem.at[0], swap_sem.at[1], sibling)
    swap.start()
    swap.wait()

    low = fin[:, 0:WINDOW]
    high = pltpu.roll(fin[:, DC - WINDOW : DC], DC // 2, 1)
    win[...] = jnp.where(k == 0, low, high)
    for share in range(8):
        wide[share, 48:PACK] = jnp.zeros((PACK - 48, WINDOW), jnp.float32)
        for m in range(3):
            if share < 7:
                lo = m * MAIN + 18 * share
                wide[share, 18 * m : 18 * m + 18] = win[lo : lo + 18]
            else:
                lo = m * MAIN + 126
                wide[share, 18 * m : 18 * m + 2] = win[lo : lo + 2]
                lo = 3 * MAIN + m * TAIL
                wide[share, 18 * m + 2 : 18 * m + 18] = win[lo : lo + TAIL]
        pack[share] = wide[share].astype(jnp.bfloat16)

    def share_copy(share):
        ty, tz = target(share)
        return remote(pack.at[share], out.at[z], send.at[share], recv.at[z], device(x, ty, tz, k))

    def start(share, carry):
        ty, tz = target(share)

        @pl.when((ty != y) | (tz != z))
        def _():
            share_copy(share).start()

        @pl.when((ty == y) & (tz == z))
        def _():
            pltpu.make_async_copy(pack.at[share], out.at[z], keep_sem).start()

        return carry

    def finish_send(share, carry):
        ty, tz = target(share)

        @pl.when((ty != y) | (tz != z))
        def _():
            share_copy(share).wait_send()

        @pl.when((ty == y) & (tz == z))
        def _():
            pltpu.make_async_copy(pack.at[share], out.at[z], keep_sem).wait()

        return carry

    def finish_recv(pz, carry):
        @pl.when((zl != y) | (pz != z))
        def _():
            pltpu.make_async_copy(out.at[pz], out.at[pz], recv.at[pz]).wait()

        return carry

    lax.fori_loop(0, 8, start, 0)
    lax.fori_loop(0, 8, finish_send, 0)
    lax.fori_loop(0, 8, finish_recv, 0)
    for off in OFFSETS:
        trades[off].wait_send()
    for go in chain.values():
        go.wait_send()


def reduce_grads(grads):
    dma = pltpu.SemaphoreType.DMA
    wide = pltpu.VMEM((EXPERTS, HALF, DC), jnp.float32)
    steps = pltpu.VMEM((2, 2, 4, QUART, DC), jnp.bfloat16)
    return pl.pallas_call(
        reduce_kernel,
        out_shape=jax.ShapeDtypeStruct((EXPERTS, PACK, WINDOW), jnp.bfloat16),
        in_specs=[pl.BlockSpec(memory_space=pl.ANY)],
        out_specs=pl.BlockSpec(memory_space=pltpu.VMEM),
        scratch_shapes=[
            wide,
            wide,
            steps,
            steps,
            pltpu.VMEM((GROWS, DC), jnp.float32),
            pltpu.VMEM((GROWS, WINDOW), jnp.float32),
            pltpu.VMEM((8, PACK, WINDOW), jnp.float32),
            pltpu.VMEM((8, PACK, WINDOW), jnp.bfloat16),
            dma((8,)),
            dma((8,)),
            dma((8,)),
            dma((16,)),
            dma((16,)),
            dma((2,)),
            dma((8,)),
            dma((8,)),
            dma,
        ],
        compiler_params=pltpu.CompilerParams(
            collective_id=1, has_side_effects=True, vmem_limit_bytes=VMEM_LIMIT
        ),
        name="reduce_grads",
    )(grads)


def on_device(tok, cot, wts, counts, column, dest, live):
    c = lax.axis_index("expert")
    in_plane = c % 8
    ids = jnp.arange(EXPERTS, dtype=jnp.int32)
    cumulative = jnp.sum(jnp.where(ids[None, :] <= ids[:, None], counts[None, :], 0), axis=1)
    first = cumulative - counts
    replicas = jnp.arange(32, dtype=jnp.int32)
    first_col = jnp.sum(jnp.where(replicas[None, :] == first[:, None], column[None, :], 0), axis=1)
    my_dest = lax.dynamic_index_in_dim(dest.reshape(X, 8, SLOT), in_plane, 1, keepdims=False)
    my_live = lax.dynamic_index_in_dim(live.reshape(X, 8), in_plane, 1, keepdims=False)
    expert = jnp.sum((cumulative[None, None, :] <= my_dest[:, :, None]).astype(jnp.int32), axis=2)
    slots = jnp.arange(SLOT, dtype=jnp.int32)
    gexp = jnp.where(slots[None, :] < my_live[:, None], expert, EXPERTS).reshape(NGRAN)

    xg, qg, hg = rows_and_hidden(first_col, gexp, tok, cot, wts)
    xg = xg.reshape(NGRAN, GRAN, DC)
    qg = qg.reshape(NGRAN, GRAN, DC)
    hg = hg.reshape(NGRAN, GRAN, LANES)
    shares = reduce_grads(gradients(gexp, xg, qg, hg))
    return shares[:, :54, : DC // 2].reshape(EXPERTS, 3, 18, DC // 2)


def solution(mesh):
    placed = (
        P("expert", "dp", None),
        P("expert", "dp", None),
        P("expert", None, None, None),
        P(),
        P(),
        P(),
        P(),
    )
    return jax.shard_map(
        on_device,
        mesh=mesh,
        in_specs=placed,
        out_specs=P(None, None, "dp", "expert"),
        check_vma=False,
    )
```

time: 251 us -> 188 us (0.75)
  Pallas kernels: 238 us -> 181 us
  local copies, waits for them, and re-layouts: 7.3 us -> 4.16 us
    pallas_call x5 -> x2, Pallas kernels: 226 us -> 169 us  [the longest x1 126 us: rows_and_hidden(): pl.pallas_call(rows_kernel, out_shape=(jax.ShapeDtypeStruct((X, SLOT, Y,...]
where the time goes in v2:
time: 188 us
  Pallas kernels  181 us (96%)
  local copies, waits for them, and re-layouts  4.16 us (2%)
  other arithmetic  3.15 us (2%)
    pallas_call x1, Pallas kernels, rows_and_hidden(): pl.pallas_call(rows_kernel, out_shape=(jax.ShapeDtypeStruct((X, SLOT, Y,...  126 us
    pallas_call x1, Pallas kernels, reduce_grads(): pl.pallas_call(reduce_kernel, out_shape=jax.ShapeDtypeStruct((EXPERTS, PA...  43.7 us
    pallas_call x1, Pallas kernels, gradients(): pl.pallas_call(grads_kernel, out_shape=jax.ShapeDtypeStruct((EXPERTS, GRO...  11.2 us

profile of v2, /device:TPU:25, one launch (start us, length us, event | category | flops | bytes accessed | tf_op | source)
XLA Modules:
  0.0 187.8 jit_solution(7062421761145606776)
XLA Ops:
  0.0 0.8 select_reduce_fusion.1
  0.8 0.7 sub.3
  1.4 1.4 select_reduce_fusion.first_col
  2.9 0.7 reshape.31
  3.6 0.2 dynamic-slice_reduce_fusion
  3.8 0.8 reshape.32
  4.5 0.1 constant_dynamic-slice_fusion
  4.6 0.1 copy.14
  4.7 0.2 convert_reduce_fusion
  5.0 0.1 fusion
  5.0 0.6 select_n.33.gexp
  5.6 125.6 %rows_and_hidden.1 = (bf16[4,8,4,16,384]{4,3,2,1,0:T(8,128)(2,1)}, bf16[4,8,4,16,384]{4,3,2,1,0:T(8,128)(2,1)}, bf16[4,8,4,16,512]{4,3,2,1,0:T(8,128)(2,1)}) custom-call(s32[8]{0:T(128)} %select_reduce_fusion.first_col, s32[32]{0:T(128)} %select_n.33.gexp, bf16[8,16,6144]{2,1,0:T(8,128)(2,1)} %tok.1, bf16[8,16,6144]{2,1,0:T(8,128)(2,1)} %cot.1, ...), custom_call_target="tpu_custom_call" | custom-call | tf_op jit(solution)/shard_map/rows_and_hidden/pallas_call | solution.py:413
  131.3 11.2 %gradients.1.grads = f32[8,448,384]{2,1,0:T(8,128)} custom-call(s32[32]{0:T(128)} %select_n.33.gexp, bf16[32,64,384]{2,1,0:T(8,128)(2,1)} %bitcast.8, bf16[32,64,384]{2,1,0:T(8,128)(2,1)} %bitcast.9, bf16[32,64,512]{2,1,0:T(8,128)(2,1)} %bitcast.7), custom_call_target="tpu_custom_call" | custom-call | tf_op jit(solution)/shard_map/gradients/pallas_call | solution.py:487
  142.5 43.7 %reduce_grads.1 = bf16[8,64,256]{2,1,0:T(8,128)(2,1)} custom-call(f32[8,448,384]{2,1,0:T(8,128)} %gradients.1.grads), custom_call_target="tpu_custom_call" | custom-call | tf_op jit(solution)/shard_map/reduce_grads/pallas_call | solution.py:666
  186.1 1.0 slice.3
  187.1 0.7 copy.13

commit v3 on v2

--- a/solution.py
+++ b/solution.py
@@ -36,9 +36,14 @@
     return (y * 2 + z // 4, (x * 4 + z % 4) * 2 + k)
 
 
+MOVES = (
+    (1, 0), (0, 1), (3, 0), (0, 3), (2, 0), (0, 2), (1, 1), (3, 3), (1, 3), (3, 1), (2, 1), (1, 2), (2, 3), (3, 2), (2, 2),
+)
+
+
 def plane_peer(x, y, step):
-    peer = (x * Y + y + step) % GROUP
-    return peer // Y, peer % Y
+    dx, dy = MOVES[step]
+    return (x + dx) % X, (y + dy) % Y
 
 
 def signal(sem, target):
@@ -61,64 +66,12 @@
     return grad * up * sig * (1.0 + gate * (1.0 - sig)), grad * act, act * up
 
 
-def place_granules(gexp, pos, owner, packed):
-    def one_expert(e, tile):
-        def one_granule(g, count):
-            hit = gexp[g] == e
-
-            @pl.when(hit)
-            def _():
-                pos[g] = tile * PER_TILE + count
-
-            return count + hit.astype(jnp.int32)
-
-        count = lax.fori_loop(0, NGRAN, one_granule, 0)
-        tiles = (count + PER_TILE - 1) // PER_TILE
-
-        def name_tile(t, carry):
-            owner[t] = e
-            return carry
-
-        lax.fori_loop(tile, tile + tiles, name_tile, 0)
-
-        def pad(g, carry):
-            at = pl.ds(pl.multiple_of(g * GRAN, GRAN), GRAN)
-            for ref in packed:
-                ref[at] = jnp.zeros((GRAN, ref.shape[1]), ref.dtype)
-            return carry
-
-        lax.fori_loop(tile * PER_TILE + count, (tile + tiles) * PER_TILE, pad, 0)
-        return tile + tiles
-
-    used = lax.fori_loop(0, EXPERTS, one_expert, 0)
-
-    def dead(g, carry):
-        @pl.when(gexp[g] >= EXPERTS)
-        def _():
-            pos[g] = MAX_TILES * PER_TILE
-
-        return carry
-
-    lax.fori_loop(0, NGRAN, dead, 0)
-    return used
-
-
 def dot_nt(a, b):
     return lax.dot_general(a, b, (((1,), (1,)), ((), ())), preferred_element_type=jnp.float32)
 
 
 def dot_tn(a, b):
     return lax.dot_general(a, b, (((0,), (0,)), ((), ())), preferred_element_type=jnp.float32)
-
-
-def sort_rows(pos, pairs):
-    def move(g, carry):
-        at = pl.ds(pl.multiple_of(pos[g] * GRAN, GRAN), GRAN)
-        for source, packed in pairs:
-            packed[at] = source[g]
-        return carry
-
-    lax.fori_loop(0, NGRAN, move, 0)
 
 
 CHUNKS = 2
@@ -127,7 +80,7 @@
 
 
 def rows_kernel(
-    first_col, gexp, tok, cot, wts, xg, qg, hg, wr, sel, wg, xv, qv, p1, r1, s2, r2, hid, xs_sem, xr_sem, qs_sem, qr_sem,
+    counts, column, dest, live, tok, cot, wts, xg, qg, hg, gexp, wr, sel, wg, xv, qv, p1, r1, s2, r2, hid, xs_sem, xr_sem, qs_sem, qr_sem,
     ws_sem, wr_sem, own_sem, rs_sem, rr_sem, ls_sem, lr_sem, ss_sem, sr_sem, p1s_sem, p1r_sem, p2s_sem, p2r_sem,
     has_sem, har_sem, hbs_sem, hbr_sem, keep_sem,
 ):
@@ -136,16 +89,13 @@
     me_col = (x * 4 + zl) * 2 + k
     barrier = pltpu.get_barrier_semaphore()
 
-    def greet_plane(step, carry):
+    def greet_column(step, carry):
+        signal(barrier, (y * 2 + zh, (me_col + step) % 32))
+        return carry
+
+    for step in range(GROUP - 1):
         px, py = plane_peer(x, y, step)
         signal(barrier, device(px, py, z, k))
-        return carry
-
-    def greet_column(step, carry):
-        signal(barrier, (y * 2 + zh, (me_col + step) % 32))
-        return carry
-
-    lax.fori_loop(1, GROUP, greet_plane, 0)
     lax.fori_loop(1, 32, greet_column, 0)
     right, left = device(x, y, (z + 1) % Z, k), device(x, y, (z + Z - 1) % Z, k)
     sibling = device(x, y, z, 1 - k)
@@ -195,23 +145,33 @@
             columns(cot, px, py), qv.at[x, :, y], qs_sem.at[step], qr_sem.at[step], device(px, py, z, k)
         )
 
-    def start_x(step, carry):
+    for step in range(GROUP - 1):
         x_copy(step).start()
-        return carry
-
-    def start_q(step, carry):
-        q_copy(step).start()
-        return carry
-
-    lax.fori_loop(1, GROUP, start_x, 0)
     own_x = pltpu.make_async_copy(columns(tok, x, y), xv.at[x, :, y], own_sem.at[0])
     own_q = pltpu.make_async_copy(columns(cot, x, y), qv.at[x, :, y], own_sem.at[1])
     own_x.start()
     own_q.start()
 
+    firsts, lasts = [], []
+    for e in range(EXPERTS):
+        firsts.append(lasts[-1] if e else 0)
+        lasts.append(firsts[-1] + counts[e])
+
+    def place_experts():
+        def one(g, carry):
+            col = ((g // SLOT) * 4 + zl) * 2 + k
+            replica = dest[col, g % SLOT]
+            expert = 0
+            for e in range(EXPERTS - 1):
+                expert += (lasts[e] <= replica).astype(jnp.int32)
+            gexp[g] = jnp.where(g % SLOT < live[col], expert, EXPERTS)
+            return carry
+
+        lax.fori_loop(0, NGRAN, one, 0)
+
     wait_bytes(wr, wr_sem)
     for e in range(EXPERTS):
-        sel[e] = wr[first_col[e]]
+        sel[e] = wr[column[firsts[e]]]
 
     def chunk(pz):
         return wg.at[:, pl.ds(pl.multiple_of((pz * 2 + k) * 32, 32), 32), :]
@@ -225,7 +185,9 @@
     rights[0].start()
     lefts[0].start()
     sibs[0].start()
-    lax.fori_loop(1, GROUP, start_q, 0)
+    for step in range(GROUP - 1):
+        q_copy(step).start()
+    place_experts()
     for t in range(1, 5):
         rights[t - 1].wait_recv()
         piece = chunk((z + Z - t) % Z)
@@ -250,18 +212,11 @@
         go.wait_recv()
     own_w.wait()
 
-    def wait_rows(step, carry):
-        x_copy(step).wait()
-        q_copy(step).wait()
-        return carry
-
-    lax.fori_loop(1, GROUP, wait_rows, 0)
+    for step in range(GROUP - 1):
+        x_copy(step).wait_recv()
     own_x.wait()
-    own_q.wait()
     keep_x = pltpu.make_async_copy(xv, xg, keep_sem.at[0])
-    keep_q = pltpu.make_async_copy(qv, qg, keep_sem.at[1])
     keep_x.start()
-    keep_q.start()
 
     a_here, b_here = x * (1 - k) + y * k, x * k + y * (1 - k)
 
@@ -275,7 +230,7 @@
     def slots(h):
         return pl.ds(h * PART, PART)
 
-    in_tail = lax.broadcasted_iota(jnp.int32, (GRAN, MAIN), 1) < 2 * TAIL
+    in_tail = lax.broadcasted_iota(jnp.int32, (ROWS, MAIN), 1) < 2 * TAIL
 
     def first_copy(h, j):
         a = (a_here + j) % 4
@@ -310,27 +265,42 @@
             plane_device(a_here, (b_here + i) % 4),
         )
 
+    def weights_of(px, s):
+        return jnp.minimum(gexp[px * SLOT + s], EXPERTS - 1)
+
+    def put_rows(px, s, lo, value):
+        for py in range(Y):
+            pa, pb = px * (1 - k) + py * k, px * k + py * (1 - k)
+            p1[pa, pb, s, :, lo : lo + value.shape[1]] = value[py * ROWS : (py + 1) * ROWS]
+
+    def project_x(g, carry):
+        px, s = g // SLOT, g % SLOT
+        e = weights_of(px, s)
+        xt = xv[px, s].reshape(GRAN, DC)
+        put_rows(px, s, 0, dot_nt(xt, wg[e, 0 : 2 * MAIN]).astype(SUM_TYPE))
+        put_rows(px, s, 3 * MAIN, dot_nt(xt, wg[e, 3 * MAIN : LANES]).astype(SUM_TYPE))
+        return carry
+
+    lax.fori_loop(0, NGRAN, project_x, 0)
+    for step in range(GROUP - 1):
+        q_copy(step).wait_recv()
+    own_q.wait()
+    keep_q = pltpu.make_async_copy(qv, qg, keep_sem.at[1])
+    keep_q.start()
     for h in range(CHUNKS):
 
-        def granule(i, carry):
+        def project_q(i, carry):
             px, s = i // PART, h * PART + i % PART
-            e = jnp.minimum(gexp[px * SLOT + s], EXPERTS - 1)
-            xt = xv[px, s].reshape(GRAN, DC)
-            qt = qv[px, s].reshape(GRAN, DC)
-            x_main = dot_nt(xt, wg[e, 0 : 2 * MAIN]).astype(SUM_TYPE)
-            x_tail = dot_nt(xt, wg[e, 3 * MAIN : LANES])
-            q_all = dot_nt(qt, wg[e, 2 * MAIN : LANES])
-            q_main = q_all[:, :MAIN].astype(SUM_TYPE)
-            tail = jnp.where(in_tail, x_tail, q_all[:, MAIN:]).astype(SUM_TYPE)
+            e = weights_of(px, s)
+            rows = dot_nt(qv[px, s].reshape(GRAN, DC), wg[e, 2 * MAIN : LANES]).astype(SUM_TYPE)
+            put_rows(px, s, 2 * MAIN, rows[:, :MAIN])
             for py in range(Y):
                 pa, pb = px * (1 - k) + py * k, px * k + py * (1 - k)
-                cut = slice(py * ROWS, (py + 1) * ROWS)
-                p1[pa, pb, s, :, 0 : 2 * MAIN] = x_main[cut]
-                p1[pa, pb, s, :, 2 * MAIN : 3 * MAIN] = q_main[cut]
-                p1[pa, pb, s, :, 3 * MAIN : LANES] = tail[cut]
+                at = (pa, pb, s, slice(None), slice(3 * MAIN, LANES))
+                p1[at] = jnp.where(in_tail, p1[at], rows[py * ROWS : (py + 1) * ROWS, MAIN:])
             return carry
 
-        lax.fori_loop(0, X * PART, granule, 0)
+        lax.fori_loop(0, X * PART, project_q, 0)
         for j in (2, 1, 3):
             first_copy(h, j).start()
 
@@ -396,6 +366,9 @@
             first_copy(h, j).wait_send()
             second_copy(h, j).wait_send()
         pltpu.make_async_copy(hid.at[slots(h)], hidden_place(a_here, b_here, h), keep_sem.at[2 + h]).wait()
+    for step in range(GROUP - 1):
+        x_copy(step).wait_send()
+        q_copy(step).wait_send()
     for go in rights + lefts + sibs:
         go.wait_send()
     wait_bytes(wr.at[pl.ds(0, 31)], ws_sem)
@@ -403,7 +376,7 @@
     keep_q.wait()
 
 
-def rows_and_hidden(first_col, gexp, tok, cot, wts):
+def rows_and_hidden(counts, column, dest, live, tok, cot, wts):
     hbm = pl.BlockSpec(memory_space=pl.ANY)
     smem = pl.BlockSpec(memory_space=pltpu.SMEM)
     dma = pltpu.SemaphoreType.DMA
@@ -416,9 +389,10 @@
             jax.ShapeDtypeStruct((X, SLOT, Y, ROWS, DC), jnp.bfloat16),
             jax.ShapeDtypeStruct((X, SLOT, Y, ROWS, DC), jnp.bfloat16),
             jax.ShapeDtypeStruct((X, SLOT, Y, ROWS, LANES), jnp.bfloat16),
+            jax.ShapeDtypeStruct((NGRAN,), jnp.int32),
         ),
-        in_specs=[smem, smem, hbm, hbm, hbm],
-        out_specs=(hbm, hbm, hbm),
+        in_specs=[smem, smem, smem, smem, hbm, hbm, hbm],
+        out_specs=(hbm, hbm, hbm, smem),
         scratch_shapes=[
             pltpu.VMEM((32, 32, DC), jnp.bfloat16),
             pltpu.VMEM((EXPERTS, 32, DC), jnp.bfloat16),
@@ -457,44 +431,95 @@
             collective_id=0, has_side_effects=True, vmem_limit_bytes=VMEM_LIMIT
         ),
         name="rows_and_hidden",
-    )(first_col, gexp, tok, cot, wts)
-
-
-def grads_kernel(gexp, xg, qg, hg, acc, xs, qs, hs, pos, owner):
-    used = place_granules(gexp, pos, owner, [xs, qs, hs])
-    sort_rows(pos, [(xg, xs), (qg, qs), (hg, hs)])
+    )(counts, column, dest, live, tok, cot, wts)
+
+
+def grads_kernel(gexp, xg, qg, hg, out, xs, qs, hs, acc, order, ends, in_sem, out_sem):
+    pairs = ((xg, xs), (qg, qs), (hg, hs))
+
+    def at(place):
+        return pl.ds(pl.multiple_of(place * GRAN, GRAN), GRAN)
+
+    def one_expert(e, tile):
+        def one_granule(g, count):
+            hit = gexp[g] == e
+
+            @pl.when(hit)
+            def _():
+                place = tile * PER_TILE + count
+                order[place] = 1
+                for i, (source, packed) in enumerate(pairs):
+                    pltpu.make_async_copy(source.at[g], packed.at[at(place)], in_sem.at[i, place]).start()
+
+            return count + hit.astype(jnp.int32)
+
+        count = lax.fori_loop(0, NGRAN, one_granule, 0)
+        tiles = (count + PER_TILE - 1) // PER_TILE
+
+        def pad(place, carry):
+            order[place] = 0
+            for _, packed in pairs:
+                packed[at(place)] = jnp.zeros((GRAN, packed.shape[1]), packed.dtype)
+            return carry
+
+        lax.fori_loop(tile * PER_TILE + count, (tile + tiles) * PER_TILE, pad, 0)
+        ends[e] = tile + tiles
+        return tile + tiles
+
+    lax.fori_loop(0, EXPERTS, one_expert, 0)
     acc[...] = jnp.zeros_like(acc)
     tail_rows = GROWS - 3 * MAIN
     from_x = lax.broadcasted_iota(jnp.int32, (tail_rows, DC), 0) < 2 * TAIL
 
-    def tile_step(t, carry):
-        at = pl.ds(pl.multiple_of(t * TILE, TILE), TILE)
-        e = owner[t]
-        xt, qt = xs[at], qs[at]
-        acc[e, 0 : 2 * MAIN] += dot_tn(hs[at, 0 : 2 * MAIN], xt)
-        acc[e, 2 * MAIN : 3 * MAIN] += dot_tn(hs[at, 2 * MAIN : 3 * MAIN], qt)
-        tail = hs[at, 3 * MAIN : LANES]
-        x_tail, q_tail = dot_tn(tail, xt), dot_tn(tail, qt)
-        acc[e, 3 * MAIN : GROWS] += jnp.where(from_x, x_tail[:tail_rows], q_tail[:tail_rows])
-        return carry
-
-    lax.fori_loop(0, used, tile_step, 0)
+    def expert_step(e, start):
+        def tile_step(t, carry):
+            for j in range(PER_TILE):
+                place = t * PER_TILE + j
+
+                @pl.when(order[place] == 1)
+                def _():
+                    for i, (source, packed) in enumerate(pairs):
+                        pltpu.make_async_copy(source.at[0], packed.at[at(place)], in_sem.at[i, place]).wait()
+
+            rows = pl.ds(pl.multiple_of(t * TILE, TILE), TILE)
+            xt, qt = xs[rows], qs[rows]
+            acc[e, 0 : 2 * MAIN] += dot_tn(hs[rows, 0 : 2 * MAIN], xt)
+            acc[e, 2 * MAIN : 3 * MAIN] += dot_tn(hs[rows, 2 * MAIN : 3 * MAIN], qt)
+            tail = hs[rows, 3 * MAIN : LANES]
+            x_tail, q_tail = dot_tn(tail, xt), dot_tn(tail, qt)
+            acc[e, 3 * MAIN : GROWS] += jnp.where(from_x, x_tail[:tail_rows], q_tail[:tail_rows])
+            return carry
+
+        lax.fori_loop(start, ends[e], tile_step, 0)
+        pltpu.make_async_copy(acc.at[e], out.at[e], out_sem.at[e]).start()
+        return ends[e]
+
+    lax.fori_loop(0, EXPERTS, expert_step, 0)
+
+    def finish(e, carry):
+        pltpu.make_async_copy(acc.at[e], out.at[e], out_sem.at[e]).wait()
+        return carry
+
+    lax.fori_loop(0, EXPERTS, finish, 0)
 
 
 def gradients(gexp, xg, qg, hg):
-    vmem = pl.BlockSpec(memory_space=pltpu.VMEM)
-    packed = (MAX_TILES + 1) * TILE
+    hbm = pl.BlockSpec(memory_space=pl.ANY)
+    packed = MAX_TILES * TILE
     return pl.pallas_call(
         grads_kernel,
         out_shape=jax.ShapeDtypeStruct((EXPERTS, GROWS, DC), jnp.float32),
-        in_specs=[pl.BlockSpec(memory_space=pltpu.SMEM), vmem, vmem, vmem],
-        out_specs=vmem,
+        in_specs=[pl.BlockSpec(memory_space=pltpu.SMEM), hbm, hbm, hbm],
+        out_specs=hbm,
         scratch_shapes=[
             pltpu.VMEM((packed, DC), jnp.bfloat16),
             pltpu.VMEM((packed, DC), jnp.bfloat16),
             pltpu.VMEM((packed, LANES), jnp.bfloat16),
-            pltpu.SMEM((NGRAN,), jnp.int32),
-            pltpu.SMEM((MAX_TILES + 1,), jnp.int32),
+            pltpu.VMEM((EXPERTS, GROWS, DC), jnp.float32),
+            pltpu.SMEM((MAX_TILES * PER_TILE,), jnp.int32),
+            pltpu.SMEM((EXPERTS,), jnp.int32),
+            pltpu.SemaphoreType.DMA((3, MAX_TILES * PER_TILE)),
+            pltpu.SemaphoreType.DMA((EXPERTS,)),
         ],
         compiler_params=pltpu.CompilerParams(vmem_limit_bytes=VMEM_LIMIT),
         name="gradients",
@@ -695,20 +720,7 @@
 
 
 def on_device(tok, cot, wts, counts, column, dest, live):
-    c = lax.axis_index("expert")
-    in_plane = c % 8
-    ids = jnp.arange(EXPERTS, dtype=jnp.int32)
-    cumulative = jnp.sum(jnp.where(ids[None, :] <= ids[:, None], counts[None, :], 0), axis=1)
-    first = cumulative - counts
-    replicas = jnp.arange(32, dtype=jnp.int32)
-    first_col = jnp.sum(jnp.where(replicas[None, :] == first[:, None], column[None, :], 0), axis=1)
-    my_dest = lax.dynamic_index_in_dim(dest.reshape(X, 8, SLOT), in_plane, 1, keepdims=False)
-    my_live = lax.dynamic_index_in_dim(live.reshape(X, 8), in_plane, 1, keepdims=False)
-    expert = jnp.sum((cumulative[None, None, :] <= my_dest[:, :, None]).astype(jnp.int32), axis=2)
-    slots = jnp.arange(SLOT, dtype=jnp.int32)
-    gexp = jnp.where(slots[None, :] < my_live[:, None], expert, EXPERTS).reshape(NGRAN)
-
-    xg, qg, hg = rows_and_hidden(first_col, gexp, tok, cot, wts)
+    xg, qg, hg, gexp = rows_and_hidden(counts, column, dest, live, tok, cot, wts)
     xg = xg.reshape(NGRAN, GRAN, DC)
     qg = qg.reshape(NGRAN, GRAN, DC)
     hg = hg.reshape(NGRAN, GRAN, LANES)

time: 188 us -> 174 us (0.926)
  Pallas kernels: 181 us -> 170 us
  other arithmetic: 3.15 us -> 0 us
    pallas_call x1, Pallas kernels: 126 us -> 115 us  [rows_and_hidden(): pl.pallas_call(rows_kernel, out_shape=(jax.ShapeDtypeStruct((X, SLOT, Y,...]
    reduce_sum x3 -> x0, other arithmetic: 2.42 us -> none  [the longest x1 1.43 us: on_device(): jnp.sum(jnp.where(replicas[None, :] == first[:, None], column[None, :], 0...]
where the time goes in v3:
time: 174 us; the launch traced here: 173 us
  Pallas kernels  170 us (98%)
  local copies, waits for them, and re-layouts  3.05 us (2%)
    pallas_call x1, Pallas kernels, rows_and_hidden(): pl.pallas_call(rows_kernel, out_shape=(jax.ShapeDtypeStruct((X, SLOT, Y,...  115 us
    pallas_call x1, Pallas kernels, reduce_grads(): pl.pallas_call(reduce_kernel, out_shape=jax.ShapeDtypeStruct((EXPERTS, PA...  43.7 us
    pallas_call x1, Pallas kernels, gradients(): pl.pallas_call(grads_kernel, out_shape=jax.ShapeDtypeStruct((EXPERTS, GRO...  11.5 us

profile of v3, /device:TPU:25, one launch (start us, length us, event | category | flops | bytes accessed | tf_op | source)
XLA Modules:
  0.0 173.3 jit_solution(7909057106160475757)
XLA Ops:
  0.0 1.4 copy.10.dest
  1.4 115.0 %rows_and_hidden.1 = (bf16[4,8,4,16,384]{4,3,2,1,0:T(8,128)(2,1)}, bf16[4,8,4,16,384]{4,3,2,1,0:T(8,128)(2,1)}, bf16[4,8,4,16,512]{4,3,2,1,0:T(8,128)(2,1)}, s32[32]{0:T(128)}) custom-call(s32[8]{0:T(128)} %counts.1, s32[32]{0:T(128)} %column.1, s32[32,8]{1,0:T(8,128)} %copy.10.dest, s32[32]{0:T(128)} %live.1, bf16[8,16,6144]{2,1,0:T(8,128)(2,1)} %tok.1, ...), custom_call_target="tpu_custom_call" | custom-call | tf_op jit(solution)/shard_map/rows_and_hidden/pallas_call | solution.py:386
  116.4 11.5 %gradients.1.grads = f32[8,448,384]{2,1,0:T(8,128)} custom-call(s32[32]{0:T(128)} %get-tuple-element.9.gexp, bf16[32,64,384]{2,1,0:T(8,128)(2,1)} %bitcast.5, bf16[32,64,384]{2,1,0:T(8,128)(2,1)} %bitcast.6, bf16[32,64,512]{2,1,0:T(8,128)(2,1)} %bitcast.4), custom_call_target="tpu_custom_call" | custom-call | tf_op jit(solution)/shard_map/gradients/pallas_call | solution.py:509
  127.9 43.7 %reduce_grads.1 = bf16[8,64,256]{2,1,0:T(8,128)(2,1)} custom-call(f32[8,448,384]{2,1,0:T(8,128)} %gradients.1.grads), custom_call_target="tpu_custom_call" | custom-call | tf_op jit(solution)/shard_map/reduce_grads/pallas_call | solution.py:691
  171.6 1.0 slice.3
  172.6 0.7 copy.11

commit v4 on v3

--- a/solution.py
+++ b/solution.py
@@ -76,11 +76,14 @@
 
 CHUNKS = 2
 PART = SLOT // CHUNKS
+PAIRS = PART // 2
+BLOCKS = 3 * PART + PAIRS
+SIDE = 64
 SUM_TYPE = jnp.float32
 
 
 def rows_kernel(
-    counts, column, dest, live, tok, cot, wts, xg, qg, hg, gexp, wr, sel, wg, xv, qv, p1, r1, s2, r2, hid, xs_sem, xr_sem, qs_sem, qr_sem,
+    counts, column, dest, live, tok, cot, wts, xg, qg, hg, gexp, wr, sel, wg, xv, qv, p1, m1, r1, s2, r2, hid, xs_sem, xr_sem, qs_sem, qr_sem,
     ws_sem, wr_sem, own_sem, rs_sem, rr_sem, ls_sem, lr_sem, ss_sem, sr_sem, p1s_sem, p1r_sem, p2s_sem, p2r_sem,
     has_sem, har_sem, hbs_sem, hbr_sem, keep_sem,
 ):
@@ -227,61 +230,85 @@
         px, py = place(a, b)
         return device(px, py, z, k)
 
-    def slots(h):
-        return pl.ds(h * PART, PART)
-
-    in_tail = lax.broadcasted_iota(jnp.int32, (ROWS, MAIN), 1) < 2 * TAIL
-
-    def first_copy(h, j):
-        a = (a_here + j) % 4
-        at = h * 3 + j - 1
-        return remote(
-            p1.at[a, :, slots(h)], r1.at[a_here, :, slots(h)], p1s_sem.at[at], p1r_sem.at[at], plane_device(a, b_here)
-        )
+    lane = lax.broadcasted_iota(jnp.int32, (ROWS, MAIN), 1)
+    place_in_side = lane % SIDE
+
+    def ahead(h):
+        return 1 if h == 0 else 3
+
+    def a_device(step):
+        return plane_device((a_here + step) % 4, b_here)
+
+    def b_device(step):
+        return plane_device(a_here, (b_here + step) % 4)
+
+    def first_copy(h, kind, src, step):
+        at = h * 3 + kind
+        return remote(src, r1.at[h, kind], p1s_sem.at[at], p1r_sem.at[at], a_device(step))
+
+    def far_copy(h):
+        return first_copy(h, 0, p1.at[(a_here + 2) % 4, h], ahead(h))
+
+    def sum_copy(h):
+        return first_copy(h, 1, m1.at[h], ahead(h))
+
+    def near_copy(h):
+        return first_copy(h, 2, p1.at[(a_here + 4 - ahead(h)) % 4, h], 4 - ahead(h))
 
     def second_copy(h, j):
         b = (b_here + j) % 4
         at = h * 3 + j - 1
-        return remote(
-            s2.at[b, slots(h)], r2.at[b_here, slots(h)], p2s_sem.at[at], p2r_sem.at[at], plane_device(a_here, b)
-        )
+        return remote(s2.at[b, h], r2.at[b_here, h], p2s_sem.at[at], p2r_sem.at[at], plane_device(a_here, b))
 
     def hidden_place(a, b, h):
         px, py = place(a, b)
-        return hg.at[px, slots(h), py]
+        return hg.at[px, py, h]
 
     def hidden_first(h, j):
         at = h * 3 + j - 1
         return remote(
-            hid.at[slots(h)], hidden_place(a_here, b_here, h), has_sem.at[at], har_sem.at[at],
-            plane_device((a_here + j) % 4, b_here),
+            hid.at[h], hidden_place(a_here, b_here, h), has_sem.at[at], har_sem.at[at], a_device(j)
         )
 
-    def hidden_second(h, j, i):
-        at = (h * 4 + j) * 3 + i - 1
+    def hidden_near(h, j, step):
+        at = (h * 4 + j) * 3 + (0 if step == 1 else 1)
         here = hidden_place((a_here + 4 - j) % 4, b_here, h)
-        return remote(
-            hid.at[slots(h)] if j == 0 else here, here, hbs_sem.at[at], hbr_sem.at[at],
-            plane_device(a_here, (b_here + i) % 4),
-        )
-
-    def weights_of(px, s):
-        return jnp.minimum(gexp[px * SLOT + s], EXPERTS - 1)
-
-    def put_rows(px, s, lo, value):
+        return remote(hid.at[h] if j == 0 else here, here, hbs_sem.at[at], hbr_sem.at[at], b_device(step))
+
+    def hidden_far(h, j):
+        at = (h * 4 + j) * 3 + 2
+        here = hidden_place((a_here + 4 - j) % 4, (b_here + 4 - ahead(h)) % 4, h)
+        return remote(here, here, hbs_sem.at[at], hbr_sem.at[at], b_device(ahead(h)))
+
+    def hidden_keep(h):
+        return pltpu.make_async_copy(hid.at[h], hidden_place(a_here, b_here, h), keep_sem.at[2 + h])
+
+    def put_rows(px, h, block, value):
         for py in range(Y):
             pa, pb = px * (1 - k) + py * k, px * k + py * (1 - k)
-            p1[pa, pb, s, :, lo : lo + value.shape[1]] = value[py * ROWS : (py + 1) * ROWS]
-
-    def project_x(g, carry):
-        px, s = g // SLOT, g % SLOT
-        e = weights_of(px, s)
-        xt = xv[px, s].reshape(GRAN, DC)
-        put_rows(px, s, 0, dot_nt(xt, wg[e, 0 : 2 * MAIN]).astype(SUM_TYPE))
-        put_rows(px, s, 3 * MAIN, dot_nt(xt, wg[e, 3 * MAIN : LANES]).astype(SUM_TYPE))
-        return carry
-
-    lax.fori_loop(0, NGRAN, project_x, 0)
+            p1[pa, h, pb, block] = value[py * ROWS : (py + 1) * ROWS].astype(SUM_TYPE)
+
+    lanes = lax.broadcasted_iota(jnp.int32, (GRAN, MAIN), 1)
+
+    def side_by_side(tails):
+        return jnp.where(lanes < SIDE, tails[0], pltpu.roll(tails[1], SIDE, 1))
+
+    def project_x(i, carry):
+        px, h, pair = i // (CHUNKS * PAIRS), (i // PAIRS) % CHUNKS, i % PAIRS
+        tails = []
+        for side in range(2):
+            at = pair + side * PAIRS
+            s = h * PART + at
+            e = jnp.minimum(gexp[px * SLOT + s], EXPERTS - 1)
+            xt = xv[px, s].reshape(GRAN, DC)
+            main = dot_nt(xt, wg[e, 0 : 2 * MAIN])
+            put_rows(px, h, 3 * at, main[:, :MAIN])
+            put_rows(px, h, 3 * at + 1, main[:, MAIN:])
+            tails.append(dot_nt(xt, wg[e, 3 * MAIN : LANES]))
+        put_rows(px, h, 3 * PART + pair, side_by_side(tails))
+        return carry
+
+    lax.fori_loop(0, X * CHUNKS * PAIRS, project_x, 0)
     for step in range(GROUP - 1):
         q_copy(step).wait_recv()
     own_q.wait()
@@ -290,82 +317,105 @@
     for h in range(CHUNKS):
 
         def project_q(i, carry):
-            px, s = i // PART, h * PART + i % PART
-            e = weights_of(px, s)
-            rows = dot_nt(qv[px, s].reshape(GRAN, DC), wg[e, 2 * MAIN : LANES]).astype(SUM_TYPE)
-            put_rows(px, s, 2 * MAIN, rows[:, :MAIN])
+            px, pair = i // PAIRS, i % PAIRS
+            tails = []
+            for side in range(2):
+                at = pair + side * PAIRS
+                s = h * PART + at
+                e = jnp.minimum(gexp[px * SLOT + s], EXPERTS - 1)
+                rows = dot_nt(qv[px, s].reshape(GRAN, DC), wg[e, 2 * MAIN : LANES])
+                put_rows(px, h, 3 * at + 2, rows[:, :MAIN])
+                tails.append(rows[:, MAIN:])
+            tail = side_by_side(tails).astype(SUM_TYPE)
             for py in range(Y):
                 pa, pb = px * (1 - k) + py * k, px * k + py * (1 - k)
-                at = (pa, pb, s, slice(None), slice(3 * MAIN, LANES))
-                p1[at] = jnp.where(in_tail, p1[at], rows[py * ROWS : (py + 1) * ROWS, MAIN:])
+                at = (pa, h, pb, 3 * PART + pair)
+                p1[at] = jnp.where(place_in_side < 2 * TAIL, p1[at], tail[py * ROWS : (py + 1) * ROWS])
             return carry
 
-        lax.fori_loop(0, X * PART, project_q, 0)
-        for j in (2, 1, 3):
-            first_copy(h, j).start()
+        lax.fori_loop(0, X * PAIRS, project_q, 0)
+        far_copy(h).start()
+        near_copy(h).start()
 
     for h in range(CHUNKS):
-        for j in (1, 2, 3):
-            first_copy(h, j).wait_recv()
+        far_copy(h).wait_recv()
+
+        def relay(b, carry):
+            m1[h, b] = p1[(a_here + ahead(h)) % 4, h, b] + r1[h, 0, b]
+            return carry
+
+        lax.fori_loop(0, 4, relay, 0)
+        sum_copy(h).start()
+
+    for h in range(CHUNKS):
+        near_copy(h).wait_recv()
+        sum_copy(h).wait_recv()
 
         def sum_first(b, carry):
-            value = p1[a_here, b, h * PART : (h + 1) * PART].astype(jnp.float32)
-            for j in (1, 2, 3):
-                value += r1[(a_here + j) % 4, b, h * PART : (h + 1) * PART].astype(jnp.float32)
-            s2[b, h * PART : (h + 1) * PART] = value
+            s2[b, h] = p1[a_here, h, b] + r1[h, 1, b] + r1[h, 2, b]
             return carry
 
         lax.fori_loop(0, 4, sum_first, 0)
         for j in (2, 1, 3):
             second_copy(h, j).start()
 
-    lane = lax.broadcasted_iota(jnp.int32, (PART * ROWS, MAIN), 1)
-
     def shift(v, amount):
         return pltpu.roll(v, amount % MAIN, 1)
 
     for h in range(CHUNKS):
         for j in (1, 2, 3):
             second_copy(h, j).wait_recv()
-        cut = slice(h * PART, (h + 1) * PART)
-
-        def total(lo):
-            value = s2[b_here, cut, :, lo : lo + MAIN]
+
+        def total(block):
+            value = s2[b_here, h, block]
             for j in (1, 2, 3):
-                value += r2[(b_here + j) % 4, cut, :, lo : lo + MAIN]
-            return value.reshape(PART * ROWS, MAIN)
-
-        def put(lo, value):
-            hid[cut, :, lo : lo + MAIN] = value.astype(jnp.bfloat16).reshape(PART, ROWS, MAIN)
-
-        for at, value in enumerate(swiglu_rows(total(0), total(MAIN), total(2 * MAIN))):
-            put(at * MAIN, value)
-        tail = total(3 * MAIN)
-        first, second, third = swiglu_rows(tail, shift(tail, -TAIL), shift(tail, -2 * TAIL))
-        packed = jnp.where(
-            lane < TAIL, first, jnp.where(lane < 2 * TAIL, shift(second, TAIL), shift(third, 2 * TAIL))
-        )
-        put(3 * MAIN, jnp.where(lane < 3 * TAIL, packed, 0.0))
+                value += r2[(b_here + j) % 4, h, block]
+            return value
+
+        for at in range(PART):
+            for m, value in enumerate(swiglu_rows(total(3 * at), total(3 * at + 1), total(3 * at + 2))):
+                hid[h, 3 * at + m] = value.astype(jnp.bfloat16)
+        for pair in range(PAIRS):
+            tail = total(3 * PART + pair)
+            first, second, third = swiglu_rows(tail, shift(tail, -TAIL), shift(tail, -2 * TAIL))
+            packed = jnp.where(
+                place_in_side < TAIL,
+                first,
+                jnp.where(place_in_side < 2 * TAIL, shift(second, TAIL), shift(third, 2 * TAIL)),
+            )
+            hid[h, 3 * PART + pair] = jnp.where(place_in_side < 3 * TAIL, packed, 0.0).astype(jnp.bfloat16)
         for j in (2, 1, 3):
             hidden_first(h, j).start()
-        for i in (2, 1, 3):
-            hidden_second(h, 0, i).start()
-        pltpu.make_async_copy(hid.at[slots(h)], hidden_place(a_here, b_here, h), keep_sem.at[2 + h]).start()
-
-    for h in range(CHUNKS):
-        for j in (1, 3, 2):
-            hidden_first(h, j).wait_recv()
-            for i in (2, 1, 3):
-                hidden_second(h, j, i).start()
+        for step in (1, 3):
+            hidden_near(h, 0, step).start()
+        hidden_keep(h).start()
+
+    arrivals = (0, 1, 3, 2)
+    for n, j in enumerate(arrivals):
+        if n + 1 < len(arrivals):
+            for h in range(CHUNKS):
+                hidden_first(h, arrivals[n + 1]).wait_recv()
+                for step in (1, 3):
+                    hidden_near(h, arrivals[n + 1], step).start()
+        for h in range(CHUNKS):
+            hidden_near(h, j, ahead(h)).wait_recv()
+            hidden_far(h, j).start()
     for h in range(CHUNKS):
         for j in range(4):
-            for i in (1, 2, 3):
-                hidden_second(h, j, i).wait()
+            hidden_near(h, j, 4 - ahead(h)).wait_recv()
+            hidden_far(h, j).wait_recv()
+    for h in range(CHUNKS):
+        for j in range(4):
+            for step in (1, 3):
+                hidden_near(h, j, step).wait_send()
+            hidden_far(h, j).wait_send()
         for j in (1, 2, 3):
             hidden_first(h, j).wait_send()
-            first_copy(h, j).wait_send()
             second_copy(h, j).wait_send()
-        pltpu.make_async_copy(hid.at[slots(h)], hidden_place(a_here, b_here, h), keep_sem.at[2 + h]).wait()
+        far_copy(h).wait_send()
+        near_copy(h).wait_send()
+        sum_copy(h).wait_send()
+        hidden_keep(h).wait()
     for step in range(GROUP - 1):
         x_copy(step).wait_send()
         q_copy(step).wait_send()
@@ -381,14 +431,15 @@
     smem = pl.BlockSpec(memory_space=pltpu.SMEM)
     dma = pltpu.SemaphoreType.DMA
     spread = pltpu.VMEM((X, SLOT, Y, ROWS, DC), jnp.bfloat16)
-    sums = pltpu.VMEM((4, 4, SLOT, ROWS, LANES), SUM_TYPE)
-    halfway = pltpu.VMEM((4, SLOT, ROWS, LANES), jnp.float32)
+    sums = pltpu.VMEM((4, CHUNKS, 4, BLOCKS, ROWS, MAIN), SUM_TYPE)
+    arrived = pltpu.VMEM((CHUNKS, 3, 4, BLOCKS, ROWS, MAIN), SUM_TYPE)
+    halfway = pltpu.VMEM((4, CHUNKS, BLOCKS, ROWS, MAIN), jnp.float32)
     return pl.pallas_call(
         rows_kernel,
         out_shape=(
             jax.ShapeDtypeStruct((X, SLOT, Y, ROWS, DC), jnp.bfloat16),
             jax.ShapeDtypeStruct((X, SLOT, Y, ROWS, DC), jnp.bfloat16),
-            jax.ShapeDtypeStruct((X, SLOT, Y, ROWS, LANES), jnp.bfloat16),
+            jax.ShapeDtypeStruct((X, Y, CHUNKS, BLOCKS, ROWS, MAIN), jnp.bfloat16),
             jax.ShapeDtypeStruct((NGRAN,), jnp.int32),
         ),
         in_specs=[smem, smem, smem, smem, hbm, hbm, hbm],
@@ -400,10 +451,11 @@
             spread,
             spread,
             sums,
-            sums,
+            pltpu.VMEM((CHUNKS, 4, BLOCKS, ROWS, MAIN), SUM_TYPE),
+            arrived,
             halfway,
             halfway,
-            pltpu.VMEM((SLOT, ROWS, LANES), jnp.bfloat16),
+            pltpu.VMEM((CHUNKS, BLOCKS, ROWS, MAIN), jnp.bfloat16),
             dma((GROUP,)),
             dma((GROUP,)),
             dma((GROUP,)),
@@ -434,70 +486,83 @@
     )(counts, column, dest, live, tok, cot, wts)
 
 
-def grads_kernel(gexp, xg, qg, hg, out, xs, qs, hs, acc, order, ends, in_sem, out_sem):
-    pairs = ((xg, xs), (qg, qs), (hg, hs))
-
-    def at(place):
-        return pl.ds(pl.multiple_of(place * GRAN, GRAN), GRAN)
-
-    def one_expert(e, tile):
-        def one_granule(g, count):
-            hit = gexp[g] == e
-
-            @pl.when(hit)
-            def _():
-                place = tile * PER_TILE + count
-                order[place] = 1
-                for i, (source, packed) in enumerate(pairs):
-                    pltpu.make_async_copy(source.at[g], packed.at[at(place)], in_sem.at[i, place]).start()
-
-            return count + hit.astype(jnp.int32)
-
-        count = lax.fori_loop(0, NGRAN, one_granule, 0)
-        tiles = (count + PER_TILE - 1) // PER_TILE
-
-        def pad(place, carry):
-            order[place] = 0
-            for _, packed in pairs:
-                packed[at(place)] = jnp.zeros((GRAN, packed.shape[1]), packed.dtype)
-            return carry
-
-        lax.fori_loop(tile * PER_TILE + count, (tile + tiles) * PER_TILE, pad, 0)
-        ends[e] = tile + tiles
-        return tile + tiles
-
-    lax.fori_loop(0, EXPERTS, one_expert, 0)
+def grads_kernel(gexp, xg, qg, hg, out, xs, qs, hs, acc, rounded, source, rank, ends, in_sem, out_sem):
+    loads = [
+        pltpu.make_async_copy(ref, held, in_sem.at[i]) for i, (ref, held) in enumerate(((hg, hs), (xg, xs), (qg, qs)))
+    ]
+    for load in loads:
+        load.start()
+
+    def clear(at, carry):
+        source[at] = -1
+        return carry
+
+    def count(g, carry):
+        e = gexp[g]
+        rank[g] = ends[e]
+        ends[e] = ends[e] + 1
+        return carry
+
+    lax.fori_loop(0, MAX_TILES * PER_TILE, clear, 0)
+    for e in range(EXPERTS + 1):
+        ends[e] = 0
+    lax.fori_loop(0, NGRAN, count, 0)
+    end = 0
+    for e in range(EXPERTS):
+        end += (ends[e] + PER_TILE - 1) // PER_TILE
+        ends[e] = end
+
+    def fill(g, carry):
+        e = gexp[g]
+
+        @pl.when(e < EXPERTS)
+        def _():
+            start = jnp.where(e > 0, ends[jnp.maximum(e - 1, 0)], 0)
+            source[start * PER_TILE + rank[g]] = g
+
+        return carry
+
+    lax.fori_loop(0, NGRAN, fill, 0)
     acc[...] = jnp.zeros_like(acc)
-    tail_rows = GROWS - 3 * MAIN
-    from_x = lax.broadcasted_iota(jnp.int32, (tail_rows, DC), 0) < 2 * TAIL
+    for load in loads:
+        load.wait()
+    tail_rows = lax.broadcasted_iota(jnp.int32, (MAIN, DC), 0) % SIDE < 2 * TAIL
+    side = lax.broadcasted_iota(jnp.int32, (ROWS, MAIN), 1) // SIDE
 
     def expert_step(e, start):
         def tile_step(t, carry):
+            xt, qt, mains, tails = [], [], ([], [], []), []
             for j in range(PER_TILE):
-                place = t * PER_TILE + j
-
-                @pl.when(order[place] == 1)
-                def _():
-                    for i, (source, packed) in enumerate(pairs):
-                        pltpu.make_async_copy(source.at[0], packed.at[at(place)], in_sem.at[i, place]).wait()
-
-            rows = pl.ds(pl.multiple_of(t * TILE, TILE), TILE)
-            xt, qt = xs[rows], qs[rows]
-            acc[e, 0 : 2 * MAIN] += dot_tn(hs[rows, 0 : 2 * MAIN], xt)
-            acc[e, 2 * MAIN : 3 * MAIN] += dot_tn(hs[rows, 2 * MAIN : 3 * MAIN], qt)
-            tail = hs[rows, 3 * MAIN : LANES]
-            x_tail, q_tail = dot_tn(tail, xt), dot_tn(tail, qt)
-            acc[e, 3 * MAIN : GROWS] += jnp.where(from_x, x_tail[:tail_rows], q_tail[:tail_rows])
+                found = source[t * PER_TILE + j]
+                g = jnp.maximum(found, 0)
+                px, h, at = g // SLOT, (g % SLOT) // PART, g % PART
+                xt.append(xs[g])
+                qt.append(qs[g])
+                for py in range(Y):
+                    for m in range(3):
+                        block = hs[px, py, h, 3 * at + m]
+                        mains[m].append(jnp.where(found >= 0, block, jnp.zeros_like(block)))
+                    block = hs[px, py, h, 3 * PART + at % PAIRS].astype(jnp.float32)
+                    mine = side == jnp.where(found >= 0, at // PAIRS, 2)
+                    tails.append(jnp.where(mine, block, 0.0).astype(jnp.bfloat16))
+            xt, qt = jnp.concatenate(xt, axis=0), jnp.concatenate(qt, axis=0)
+            for m, rows in ((0, xt), (1, xt), (2, qt)):
+                acc[e, m * MAIN : (m + 1) * MAIN] += dot_tn(jnp.concatenate(mains[m], axis=0), rows)
+            tail = jnp.concatenate(tails, axis=0)
+            both = jnp.where(tail_rows, dot_tn(tail, xt), dot_tn(tail, qt))
+            acc[e, 3 * MAIN : GROWS] += both[:SIDE] + both[SIDE:]
             return carry
 
-        lax.fori_loop(start, ends[e], tile_step, 0)
-        pltpu.make_async_copy(acc.at[e], out.at[e], out_sem.at[e]).start()
-        return ends[e]
+        end = ends[e]
+        lax.fori_loop(start, end, tile_step, 0)
+        rounded[e] = acc[e].astype(jnp.bfloat16)
+        pltpu.make_async_copy(rounded.at[e], out.at[e], out_sem.at[e]).start()
+        return end
 
     lax.fori_loop(0, EXPERTS, expert_step, 0)
 
     def finish(e, carry):
-        pltpu.make_async_copy(acc.at[e], out.at[e], out_sem.at[e]).wait()
+        pltpu.make_async_copy(rounded.at[e], out.at[e], out_sem.at[e]).wait()
         return carry
 
     lax.fori_loop(0, EXPERTS, finish, 0)
@@ -505,20 +570,21 @@
 
 def gradients(gexp, xg, qg, hg):
     hbm = pl.BlockSpec(memory_space=pl.ANY)
-    packed = MAX_TILES * TILE
     return pl.pallas_call(
         grads_kernel,
-        out_shape=jax.ShapeDtypeStruct((EXPERTS, GROWS, DC), jnp.float32),
+        out_shape=jax.ShapeDtypeStruct((EXPERTS, GROWS, DC), jnp.bfloat16),
         in_specs=[pl.BlockSpec(memory_space=pltpu.SMEM), hbm, hbm, hbm],
         out_specs=hbm,
         scratch_shapes=[
-            pltpu.VMEM((packed, DC), jnp.bfloat16),
-            pltpu.VMEM((packed, DC), jnp.bfloat16),
-            pltpu.VMEM((packed, LANES), jnp.bfloat16),
+            pltpu.VMEM(xg.shape, jnp.bfloat16),
+            pltpu.VMEM(qg.shape, jnp.bfloat16),
+            pltpu.VMEM(hg.shape, jnp.bfloat16),
             pltpu.VMEM((EXPERTS, GROWS, DC), jnp.float32),
+            pltpu.VMEM((EXPERTS, GROWS, DC), jnp.bfloat16),
             pltpu.SMEM((MAX_TILES * PER_TILE,), jnp.int32),
-            pltpu.SMEM((EXPERTS,), jnp.int32),
-            pltpu.SemaphoreType.DMA((3, MAX_TILES * PER_TILE)),
+            pltpu.SMEM((NGRAN,), jnp.int32),
+            pltpu.SMEM((EXPERTS + 1,), jnp.int32),
+            pltpu.SemaphoreType.DMA((3,)),
             pltpu.SemaphoreType.DMA((EXPERTS,)),
         ],
         compiler_params=pltpu.CompilerParams(vmem_limit_bytes=VMEM_LIMIT),
@@ -527,13 +593,14 @@
 
 
 QUART = HALF // 2
-PACK = 64
+PACK = 96
+SHARE = 54
 WINDOW = 256
 OFFSETS = (4, 3, -3, 2, -2, 1, -1, 0)
 
 
 def reduce_kernel(
-    grads, out, own, sib, sbuf, rbuf, fin, win, wide, pack, os_sem, ts_sem, tr_sem, cs_sem, cr_sem, swap_sem, send, recv,
+    grads, out, own, sib, sbuf, rbuf, fin, win, wide, packf, pack, got, gotf, os_sem, ts_sem, tr_sem, cs_sem, cr_sem, swap_sem, send, recv,
     keep_sem,
 ):
     x, y, z, k = coords()
@@ -591,7 +658,7 @@
             ready.add(off)
         e = (z + off + Z) % Z
         cut = slice(j * QUART, (j + 1) * QUART)
-        return own[e, cut] + sib[e, cut]
+        return own[e, cut].astype(jnp.float32) + sib[e, cut].astype(jnp.float32)
 
     chain = {}
     for dist in (4, 3, 2, 1):
@@ -625,8 +692,8 @@
     low = fin[:, 0:WINDOW]
     high = pltpu.roll(fin[:, DC - WINDOW : DC], DC // 2, 1)
     win[...] = jnp.where(k == 0, low, high)
+    first_half = lax.broadcasted_iota(jnp.int32, (SHARE // 2, MAIN), 1) < SIDE
     for share in range(8):
-        wide[share, 48:PACK] = jnp.zeros((PACK - 48, WINDOW), jnp.float32)
         for m in range(3):
             if share < 7:
                 lo = m * MAIN + 18 * share
@@ -636,11 +703,18 @@
                 wide[share, 18 * m : 18 * m + 2] = win[lo : lo + 2]
                 lo = 3 * MAIN + m * TAIL
                 wide[share, 18 * m + 2 : 18 * m + 18] = win[lo : lo + TAIL]
-        pack[share] = wide[share].astype(jnp.bfloat16)
+        packf[share, 80:PACK] = jnp.zeros((PACK - 80, MAIN), jnp.float32)
+        packf[share, 0:SHARE] = wide[share, 0:SHARE, :MAIN]
+        packf[share, SHARE : SHARE + SHARE // 2] = jnp.where(
+            first_half,
+            wide[share, 0 : SHARE // 2, MAIN:],
+            pltpu.roll(wide[share, SHARE // 2 : SHARE, MAIN:], SIDE, 1),
+        )
+        pack[share] = packf[share].astype(jnp.bfloat16)
 
     def share_copy(share):
         ty, tz = target(share)
-        return remote(pack.at[share], out.at[z], send.at[share], recv.at[z], device(x, ty, tz, k))
+        return remote(pack.at[share], got.at[z], send.at[share], recv.at[z], device(x, ty, tz, k))
 
     def start(share, carry):
         ty, tz = target(share)
@@ -651,7 +725,7 @@
 
         @pl.when((ty == y) & (tz == z))
         def _():
-            pltpu.make_async_copy(pack.at[share], out.at[z], keep_sem).start()
+            pltpu.make_async_copy(pack.at[share], got.at[z], keep_sem).start()
 
         return carry
 
@@ -664,20 +738,30 @@
 
         @pl.when((ty == y) & (tz == z))
         def _():
-            pltpu.make_async_copy(pack.at[share], out.at[z], keep_sem).wait()
+            pltpu.make_async_copy(pack.at[share], got.at[z], keep_sem).wait()
 
         return carry
 
     def finish_recv(pz, carry):
         @pl.when((zl != y) | (pz != z))
         def _():
-            pltpu.make_async_copy(out.at[pz], out.at[pz], recv.at[pz]).wait()
+            pltpu.make_async_copy(got.at[pz], got.at[pz], recv.at[pz]).wait()
 
         return carry
 
     lax.fori_loop(0, 8, start, 0)
     lax.fori_loop(0, 8, finish_send, 0)
+    def unpack(e, carry):
+        value = got[e].astype(jnp.float32)
+        gotf[0:PACK, :MAIN] = value
+        gotf[0 : SHARE // 2, MAIN:] = gotf[SHARE : SHARE + SHARE // 2, :MAIN]
+        gotf[SHARE // 2 : SHARE, MAIN:] = pltpu.roll(gotf[SHARE : SHARE + SHARE // 2, :MAIN], SIDE, 1)
+        for m in range(3):
+            out[e, m] = gotf[18 * m : 18 * m + 18, : DC // 2].astype(jnp.bfloat16)
+        return carry
+
     lax.fori_loop(0, 8, finish_recv, 0)
+    lax.fori_loop(0, 8, unpack, 0)
     for off in OFFSETS:
         trades[off].wait_send()
     for go in chain.values():
@@ -686,11 +770,11 @@
 
 def reduce_grads(grads):
     dma = pltpu.SemaphoreType.DMA
-    wide = pltpu.VMEM((EXPERTS, HALF, DC), jnp.float32)
+    wide = pltpu.VMEM((EXPERTS, HALF, DC), jnp.bfloat16)
     steps = pltpu.VMEM((2, 2, 4, QUART, DC), jnp.bfloat16)
     return pl.pallas_call(
         reduce_kernel,
-        out_shape=jax.ShapeDtypeStruct((EXPERTS, PACK, WINDOW), jnp.bfloat16),
+        out_shape=jax.ShapeDtypeStruct((EXPERTS, 3, 18, DC // 2), jnp.bfloat16),
         in_specs=[pl.BlockSpec(memory_space=pl.ANY)],
         out_specs=pl.BlockSpec(memory_space=pltpu.VMEM),
         scratch_shapes=[
@@ -700,8 +784,11 @@
             steps,
             pltpu.VMEM((GROWS, DC), jnp.float32),
             pltpu.VMEM((GROWS, WINDOW), jnp.float32),
-            pltpu.VMEM((8, PACK, WINDOW), jnp.float32),
-            pltpu.VMEM((8, PACK, WINDOW), jnp.bfloat16),
+            pltpu.VMEM((8, SHARE + 2, WINDOW), jnp.float32),
+            pltpu.VMEM((8, PACK, MAIN), jnp.float32),
+            pltpu.VMEM((8, PACK, MAIN), jnp.bfloat16),
+            pltpu.VMEM((8, PACK, MAIN), jnp.bfloat16),
+            pltpu.VMEM((PACK, WINDOW), jnp.float32),
             dma((8,)),
             dma((8,)),
             dma((8,)),
@@ -723,9 +810,7 @@
     xg, qg, hg, gexp = rows_and_hidden(counts, column, dest, live, tok, cot, wts)
     xg = xg.reshape(NGRAN, GRAN, DC)
     qg = qg.reshape(NGRAN, GRAN, DC)
-    hg = hg.reshape(NGRAN, GRAN, LANES)
-    shares = reduce_grads(gradients(gexp, xg, qg, hg))
-    return shares[:, :54, : DC // 2].reshape(EXPERTS, 3, 18, DC // 2)
+    return reduce_grads(gradients(gexp, xg, qg, hg))
 
 
 def solution(mesh):

time: 174 us -> 164 us (0.943)
  Pallas kernels: 170 us -> 161 us
    pallas_call x1, Pallas kernels: 115 us -> 104 us  [rows_and_hidden(): pl.pallas_call(rows_kernel, out_shape=(jax.ShapeDtypeStruct((X, SLOT, Y,...]
    pallas_call x1, Pallas kernels: 43.7 us -> 49.1 us  [reduce_grads(): pl.pallas_call(reduce_kernel, out_shape=jax.ShapeDtypeStruct((EXPERTS, 3,...]
    pallas_call x1, Pallas kernels: 11.5 us -> 7.54 us  [gradients(): pl.pallas_call(grads_kernel, out_shape=jax.ShapeDtypeStruct((EXPERTS, GRO...]
where the time goes in v4:
time: 164 us
  Pallas kernels  161 us (98%)
  local copies, waits for them, and re-layouts  3.05 us (2%)
    pallas_call x1, Pallas kernels, rows_and_hidden(): pl.pallas_call(rows_kernel, out_shape=(jax.ShapeDtypeStruct((X, SLOT, Y,...  104 us
    pallas_call x1, Pallas kernels, reduce_grads(): pl.pallas_call(reduce_kernel, out_shape=jax.ShapeDtypeStruct((EXPERTS, 3,...  49.1 us
    pallas_call x1, Pallas kernels, gradients(): pl.pallas_call(grads_kernel, out_shape=jax.ShapeDtypeStruct((EXPERTS, GRO...  7.54 us

profile of v4, /device:TPU:25, one launch (start us, length us, event | category | flops | bytes accessed | tf_op | source)
XLA Modules:
  0.0 164.0 jit_solution(6620748504578335254)
XLA Ops:
  0.0 1.4 copy.8.dest
  1.4 104.3 %rows_and_hidden.1 = (bf16[4,8,4,16,384]{4,3,2,1,0:T(8,128)(2,1)}, bf16[4,8,4,16,384]{4,3,2,1,0:T(8,128)(2,1)}, bf16[4,4,2,14,16,128]{5,4,3,2,1,0:T(8,128)(2,1)}, s32[32]{0:T(128)}) custom-call(s32[8]{0:T(128)} %counts.1, s32[32]{0:T(128)} %column.1, s32[32,8]{1,0:T(8,128)} %copy.8.dest, s32[32]{0:T(128)} %live.1, bf16[8,16,6144]{2,1,0:T(8,128)(2,1)} %tok.1, ...), custom_call_target="tpu_custom_call" | custom-call | tf_op jit(solution)/shard_map/rows_and_hidden/pallas_call | solution.py:437
  105.7 7.5 %gradients.1.grads = bf16[8,448,384]{2,1,0:T(8,128)(2,1)} custom-call(s32[32]{0:T(128)} %get-tuple-element.9.gexp, bf16[32,64,384]{2,1,0:T(8,128)(2,1)} %bitcast.2, bf16[32,64,384]{2,1,0:T(8,128)(2,1)} %bitcast.3, bf16[4,4,2,14,16,128]{5,4,3,2,1,0:T(8,128)(2,1)} %get-tuple-element.12.hg), custom_call_target="tpu_custom_call" | custom-call | tf_op jit(solution)/shard_map/gradients/pallas_call | solution.py:573
  113.2 49.1 %reduce_grads.1 = bf16[8,3,18,192]{3,2,1,0:T(8,128)(2,1)} custom-call(bf16[8,448,384]{2,1,0:T(8,128)(2,1)} %gradients.1.grads), custom_call_target="tpu_custom_call" | custom-call | tf_op jit(solution)/shard_map/reduce_grads/pallas_call | solution.py:775
  162.3 1.7 %copy.9 = bf16[8,3,18,192]{3,0,2,1:T(8,128)(2,1)} copy(bf16[8,3,18,192]{3,2,1,0:T(8,128)(2,1)} %reduce_grads.1) | data formatting | bytes 331776 | tf_op jit(solution)/shard_map/reduce_grads/pallas_call | solution.py:775

commit v5 on v4

--- a/solution.py
+++ b/solution.py
@@ -79,35 +79,42 @@
 PAIRS = PART // 2
 BLOCKS = 3 * PART + PAIRS
 SIDE = 64
-SUM_TYPE = jnp.float32
 
 
 def rows_kernel(
-    counts, column, dest, live, tok, cot, wts, xg, qg, hg, gexp, wr, sel, wg, xv, qv, p1, m1, r1, s2, r2, hid, xs_sem, xr_sem, qs_sem, qr_sem,
+    counts, column, dest, live, tok, cot, wts, xg, qg, hg, gexp, wr, sel, wg, xv, qv, pg, mg, rg, sg, tg,
+    pq, mq, rq, sq, tq, hid, xs_sem, xr_sem, qs_sem, qr_sem,
     ws_sem, wr_sem, own_sem, rs_sem, rr_sem, ls_sem, lr_sem, ss_sem, sr_sem, p1s_sem, p1r_sem, p2s_sem, p2r_sem,
     has_sem, har_sem, hbs_sem, hbr_sem, keep_sem,
 ):
     x, y, z, k = coords()
-    zh, zl = z // 4, z % 4
+    zl = z % 4
     me_col = (x * 4 + zl) * 2 + k
     barrier = pltpu.get_barrier_semaphore()
 
-    def greet_column(step, carry):
-        signal(barrier, (y * 2 + zh, (me_col + step) % 32))
+    def greet_copies(dx, carry):
+        cx = (x + dx) % X
+        for dz in (0, 1, 7, 2, 6):
+            for ck in range(2):
+                if dz == 0:
+
+                    @pl.when((dx > 0) | (k != ck))
+                    def _():
+                        signal(barrier, device(cx, y, z, ck))
+
+                else:
+                    signal(barrier, device(cx, y, (z + dz) % Z, ck))
         return carry
 
     for step in range(GROUP - 1):
         px, py = plane_peer(x, y, step)
         signal(barrier, device(px, py, z, k))
-    lax.fori_loop(1, 32, greet_column, 0)
+    lax.fori_loop(0, X, greet_copies, 0)
     right, left = device(x, y, (z + 1) % Z, k), device(x, y, (z + Z - 1) % Z, k)
     sibling = device(x, y, z, 1 - k)
-    signal(barrier, right)
-    signal(barrier, left)
-    pl.semaphore_wait(barrier, GROUP - 1 + 31 + 2)
-
-    def weight_piece(col, part):
-        cx, cz, ck = col // 8, zh * 4 + (col // 2) % 4, col % 2
+    pl.semaphore_wait(barrier, GROUP - 1 + 39)
+
+    def weight_piece(cx, cz, ck, part):
         t = jnp.minimum((cz * 2 + ck) * 2 + part, 26)
         tail = t // 24
         m = (t // 8) * (1 - tail) + (t - 24) * tail
@@ -119,18 +126,34 @@
             pl.ds(pl.multiple_of((cx * Y + y) * DC, 128), DC),
         ]
 
-    def send_weights(step, carry):
-        col = (me_col + step) % 32
-        for part in range(2):
-            remote(
-                weight_piece(col, part), wr.at[me_col, pl.ds(part * 16, 16), :], ws_sem, wr_sem, (y * 2 + zh, col)
-            ).start()
-        return carry
-
-    lax.fori_loop(1, 32, send_weights, 0)
+    def send_weights(dx, carry):
+        cx = (x + dx) % X
+
+        def send(cz, ck):
+            for part in range(2):
+                remote(
+                    weight_piece(cx, cz, ck, part),
+                    wr.at[me_col, pl.ds(part * 16, 16), :],
+                    ws_sem,
+                    wr_sem,
+                    device(cx, y, cz, ck),
+                ).start()
+
+        for dz, ck in ((2, 0), (6, 1), (1, 0), (7, 0), (1, 1), (7, 1), (0, 0), (0, 1)):
+            if dz == 0:
+
+                @pl.when((dx > 0) | (k != ck))
+                def _():
+                    send(z, ck)
+
+            else:
+                send((z + dz) % Z, ck)
+        return carry
+
+    lax.fori_loop(0, X, send_weights, 0)
     for part in range(2):
         pltpu.make_async_copy(
-            weight_piece(me_col, part), wr.at[me_col, pl.ds(part * 16, 16), :], wr_sem
+            weight_piece(x, z, k, part), wr.at[me_col, pl.ds(part * 16, 16), :], wr_sem
         ).start()
 
     def columns(ref, px, py):
@@ -242,23 +265,27 @@
     def b_device(step):
         return plane_device(a_here, (b_here + step) % 4)
 
-    def first_copy(h, kind, src, step):
-        at = h * 3 + kind
-        return remote(src, r1.at[h, kind], p1s_sem.at[at], p1r_sem.at[at], a_device(step))
-
-    def far_copy(h):
-        return first_copy(h, 0, p1.at[(a_here + 2) % 4, h], ahead(h))
-
-    def sum_copy(h):
-        return first_copy(h, 1, m1.at[h], ahead(h))
-
-    def near_copy(h):
-        return first_copy(h, 2, p1.at[(a_here + 4 - ahead(h)) % 4, h], 4 - ahead(h))
-
-    def second_copy(h, j):
+    parts = ((pg, mg, rg, sg, tg), (pq, mq, rq, sq, tq))
+
+    def first_copy(c, kind, src, step):
+        at = c * 3 + kind
+        return remote(src, parts[c][2].at[kind], p1s_sem.at[at], p1r_sem.at[at], a_device(step))
+
+    def far_copy(c):
+        return first_copy(c, 0, parts[c][0].at[(a_here + 2) % 4], ahead(c))
+
+    def sum_copy(c):
+        return first_copy(c, 1, parts[c][1], ahead(c))
+
+    def near_copy(c):
+        return first_copy(c, 2, parts[c][0].at[(a_here + 4 - ahead(c)) % 4], 4 - ahead(c))
+
+    def second_copy(c, j):
         b = (b_here + j) % 4
-        at = h * 3 + j - 1
-        return remote(s2.at[b, h], r2.at[b_here, h], p2s_sem.at[at], p2r_sem.at[at], plane_device(a_here, b))
+        at = c * 3 + j - 1
+        return remote(
+            parts[c][3].at[b], parts[c][4].at[b_here], p2s_sem.at[at], p2r_sem.at[at], plane_device(a_here, b)
+        )
 
     def hidden_place(a, b, h):
         px, py = place(a, b)
@@ -283,10 +310,10 @@
     def hidden_keep(h):
         return pltpu.make_async_copy(hid.at[h], hidden_place(a_here, b_here, h), keep_sem.at[2 + h])
 
-    def put_rows(px, h, block, value):
+    def put_rows(ref, px, block, value):
         for py in range(Y):
             pa, pb = px * (1 - k) + py * k, px * k + py * (1 - k)
-            p1[pa, h, pb, block] = value[py * ROWS : (py + 1) * ROWS].astype(SUM_TYPE)
+            ref[pa, pb, block] = value[py * ROWS : (py + 1) * ROWS]
 
     lanes = lax.broadcasted_iota(jnp.int32, (GRAN, MAIN), 1)
 
@@ -294,89 +321,95 @@
         return jnp.where(lanes < SIDE, tails[0], pltpu.roll(tails[1], SIDE, 1))
 
     def project_x(i, carry):
-        px, h, pair = i // (CHUNKS * PAIRS), (i // PAIRS) % CHUNKS, i % PAIRS
+        px, pair = i // (CHUNKS * PAIRS), i % (CHUNKS * PAIRS)
         tails = []
         for side in range(2):
-            at = pair + side * PAIRS
-            s = h * PART + at
+            s = (pair // PAIRS) * PART + pair % PAIRS + side * PAIRS
             e = jnp.minimum(gexp[px * SLOT + s], EXPERTS - 1)
             xt = xv[px, s].reshape(GRAN, DC)
             main = dot_nt(xt, wg[e, 0 : 2 * MAIN])
-            put_rows(px, h, 3 * at, main[:, :MAIN])
-            put_rows(px, h, 3 * at + 1, main[:, MAIN:])
+            put_rows(pg, px, s, main[:, :MAIN])
+            put_rows(pg, px, SLOT + s, main[:, MAIN:])
             tails.append(dot_nt(xt, wg[e, 3 * MAIN : LANES]))
-        put_rows(px, h, 3 * PART + pair, side_by_side(tails))
-        return carry
+        put_rows(pq, px, SLOT + pair, side_by_side(tails))
+        return carry
+
+    def project_q(i, carry):
+        px, pair = i // (CHUNKS * PAIRS), i % (CHUNKS * PAIRS)
+        tails = []
+        for side in range(2):
+            s = (pair // PAIRS) * PART + pair % PAIRS + side * PAIRS
+            e = jnp.minimum(gexp[px * SLOT + s], EXPERTS - 1)
+            rows = dot_nt(qv[px, s].reshape(GRAN, DC), wg[e, 2 * MAIN : LANES])
+            put_rows(pq, px, s, rows[:, :MAIN])
+            tails.append(rows[:, MAIN:])
+        tail = side_by_side(tails)
+        for py in range(Y):
+            pa, pb = px * (1 - k) + py * k, px * k + py * (1 - k)
+            at = (pa, pb, SLOT + pair)
+            pq[at] = jnp.where(place_in_side < 2 * TAIL, pq[at], tail[py * ROWS : (py + 1) * ROWS])
+        return carry
+
+    def relay(c):
+        mine, passed, came = parts[c][:3]
+
+        def one(b, carry):
+            passed[b] = mine[(a_here + ahead(c)) % 4, b] + came[0, b]
+            return carry
+
+        far_copy(c).wait_recv()
+        lax.fori_loop(0, 4, one, 0)
+        sum_copy(c).start()
+
+    def add_up(c):
+        mine, _, came, sums, _ = parts[c]
+
+        def one(b, carry):
+            sums[b] = mine[a_here, b] + came[1, b] + came[2, b]
+            return carry
+
+        near_copy(c).wait_recv()
+        sum_copy(c).wait_recv()
+        lax.fori_loop(0, 4, one, 0)
+        for j in (2, 1, 3):
+            second_copy(c, j).start()
 
     lax.fori_loop(0, X * CHUNKS * PAIRS, project_x, 0)
+    far_copy(0).start()
+    near_copy(0).start()
+    relay(0)
     for step in range(GROUP - 1):
         q_copy(step).wait_recv()
     own_q.wait()
     keep_q = pltpu.make_async_copy(qv, qg, keep_sem.at[1])
     keep_q.start()
-    for h in range(CHUNKS):
-
-        def project_q(i, carry):
-            px, pair = i // PAIRS, i % PAIRS
-            tails = []
-            for side in range(2):
-                at = pair + side * PAIRS
-                s = h * PART + at
-                e = jnp.minimum(gexp[px * SLOT + s], EXPERTS - 1)
-                rows = dot_nt(qv[px, s].reshape(GRAN, DC), wg[e, 2 * MAIN : LANES])
-                put_rows(px, h, 3 * at + 2, rows[:, :MAIN])
-                tails.append(rows[:, MAIN:])
-            tail = side_by_side(tails).astype(SUM_TYPE)
-            for py in range(Y):
-                pa, pb = px * (1 - k) + py * k, px * k + py * (1 - k)
-                at = (pa, h, pb, 3 * PART + pair)
-                p1[at] = jnp.where(place_in_side < 2 * TAIL, p1[at], tail[py * ROWS : (py + 1) * ROWS])
-            return carry
-
-        lax.fori_loop(0, X * PAIRS, project_q, 0)
-        far_copy(h).start()
-        near_copy(h).start()
-
-    for h in range(CHUNKS):
-        far_copy(h).wait_recv()
-
-        def relay(b, carry):
-            m1[h, b] = p1[(a_here + ahead(h)) % 4, h, b] + r1[h, 0, b]
-            return carry
-
-        lax.fori_loop(0, 4, relay, 0)
-        sum_copy(h).start()
-
-    for h in range(CHUNKS):
-        near_copy(h).wait_recv()
-        sum_copy(h).wait_recv()
-
-        def sum_first(b, carry):
-            s2[b, h] = p1[a_here, h, b] + r1[h, 1, b] + r1[h, 2, b]
-            return carry
-
-        lax.fori_loop(0, 4, sum_first, 0)
-        for j in (2, 1, 3):
-            second_copy(h, j).start()
+    lax.fori_loop(0, X * CHUNKS * PAIRS, project_q, 0)
+    far_copy(1).start()
+    near_copy(1).start()
+    add_up(0)
+    relay(1)
+    add_up(1)
 
     def shift(v, amount):
         return pltpu.roll(v, amount % MAIN, 1)
 
+    for c in range(2):
+        for j in (1, 2, 3):
+            second_copy(c, j).wait_recv()
+
+    def total(c, block):
+        value = parts[c][3][b_here, block]
+        for j in (1, 2, 3):
+            value += parts[c][4][(b_here + j) % 4, block]
+        return value
+
     for h in range(CHUNKS):
-        for j in (1, 2, 3):
-            second_copy(h, j).wait_recv()
-
-        def total(block):
-            value = s2[b_here, h, block]
-            for j in (1, 2, 3):
-                value += r2[(b_here + j) % 4, h, block]
-            return value
-
         for at in range(PART):
-            for m, value in enumerate(swiglu_rows(total(3 * at), total(3 * at + 1), total(3 * at + 2))):
+            s = h * PART + at
+            for m, value in enumerate(swiglu_rows(total(0, s), total(0, SLOT + s), total(1, s))):
                 hid[h, 3 * at + m] = value.astype(jnp.bfloat16)
         for pair in range(PAIRS):
-            tail = total(3 * PART + pair)
+            tail = total(1, SLOT + h * PAIRS + pair)
             first, second, third = swiglu_rows(tail, shift(tail, -TAIL), shift(tail, -2 * TAIL))
             packed = jnp.where(
                 place_in_side < TAIL,
@@ -431,9 +464,10 @@
     smem = pl.BlockSpec(memory_space=pltpu.SMEM)
     dma = pltpu.SemaphoreType.DMA
     spread = pltpu.VMEM((X, SLOT, Y, ROWS, DC), jnp.bfloat16)
-    sums = pltpu.VMEM((4, CHUNKS, 4, BLOCKS, ROWS, MAIN), SUM_TYPE)
-    arrived = pltpu.VMEM((CHUNKS, 3, 4, BLOCKS, ROWS, MAIN), SUM_TYPE)
-    halfway = pltpu.VMEM((4, CHUNKS, BLOCKS, ROWS, MAIN), jnp.float32)
+    sums = []
+    for blocks in (2 * SLOT, SLOT + CHUNKS * PAIRS):
+        for lead in ((4, 4), (4,), (3, 4), (4,), (4,)):
+            sums.append(pltpu.VMEM((*lead, blocks, ROWS, MAIN), jnp.float32))
     return pl.pallas_call(
         rows_kernel,
         out_shape=(
@@ -450,11 +484,7 @@
             pltpu.VMEM((EXPERTS, LANES, DC), jnp.bfloat16),
             spread,
             spread,
-            sums,
-            pltpu.VMEM((CHUNKS, 4, BLOCKS, ROWS, MAIN), SUM_TYPE),
-            arrived,
-            halfway,
-            halfway,
+            *sums,
             pltpu.VMEM((CHUNKS, BLOCKS, ROWS, MAIN), jnp.bfloat16),
             dma((GROUP,)),
             dma((GROUP,)),

time: 164 us -> 169 us (1.030)
  Pallas kernels: 161 us -> 165 us
    pallas_call x1, Pallas kernels: 104 us -> 107 us  [rows_and_hidden(): pl.pallas_call(rows_kernel, out_shape=(jax.ShapeDtypeStruct((X, SLOT, Y,...]
where the time goes in v5:
time: 169 us; the launch traced here: 168 us
  Pallas kernels  165 us (98%)
  local copies, waits for them, and re-layouts  3.05 us (2%)
    pallas_call x1, Pallas kernels, rows_and_hidden(): pl.pallas_call(rows_kernel, out_shape=(jax.ShapeDtypeStruct((X, SLOT, Y,...  107 us
    pallas_call x1, Pallas kernels, reduce_grads(): pl.pallas_call(reduce_kernel, out_shape=jax.ShapeDtypeStruct((EXPERTS, 3,...  50.4 us
    pallas_call x1, Pallas kernels, gradients(): pl.pallas_call(grads_kernel, out_shape=jax.ShapeDtypeStruct((EXPERTS, GRO...  7.95 us

profile of v5, /device:TPU:25, one launch (start us, length us, event | category | flops | bytes accessed | tf_op | source)
XLA Modules:
  0.0 168.4 jit_solution(2416536336037084551)
XLA Ops:
  0.0 1.4 copy.8.dest
  1.4 107.0 %rows_and_hidden.1 = (bf16[4,8,4,16,384]{4,3,2,1,0:T(8,128)(2,1)}, bf16[4,8,4,16,384]{4,3,2,1,0:T(8,128)(2,1)}, bf16[4,4,2,14,16,128]{5,4,3,2,1,0:T(8,128)(2,1)}, s32[32]{0:T(128)}) custom-call(s32[8]{0:T(128)} %counts.1, s32[32]{0:T(128)} %column.1, s32[32,8]{1,0:T(8,128)} %copy.8.dest, s32[32]{0:T(128)} %live.1, bf16[8,16,6144]{2,1,0:T(8,128)(2,1)} %tok.1, ...), custom_call_target="tpu_custom_call" | custom-call | tf_op jit(solution)/shard_map/rows_and_hidden/pallas_call | solution.py:471
  108.4 8.0 %gradients.1.grads = bf16[8,448,384]{2,1,0:T(8,128)(2,1)} custom-call(s32[32]{0:T(128)} %get-tuple-element.9.gexp, bf16[32,64,384]{2,1,0:T(8,128)(2,1)} %bitcast.2, bf16[32,64,384]{2,1,0:T(8,128)(2,1)} %bitcast.3, bf16[4,4,2,14,16,128]{5,4,3,2,1,0:T(8,128)(2,1)} %get-tuple-element.12.hg), custom_call_target="tpu_custom_call" | custom-call | tf_op jit(solution)/shard_map/gradients/pallas_call | solution.py:603
  116.3 50.4 %reduce_grads.1 = bf16[8,3,18,192]{3,2,1,0:T(8,128)(2,1)} custom-call(bf16[8,448,384]{2,1,0:T(8,128)(2,1)} %gradients.1.grads), custom_call_target="tpu_custom_call" | custom-call | tf_op jit(solution)/shard_map/reduce_grads/pallas_call | solution.py:805
  166.7 1.7 %copy.9 = bf16[8,3,18,192]{3,0,2,1:T(8,128)(2,1)} copy(bf16[8,3,18,192]{3,2,1,0:T(8,128)(2,1)} %reduce_grads.1) | data formatting | bytes 331776 | tf_op jit(solution)/shard_map/reduce_grads/pallas_call | solution.py:805

commit v6 on v4

--- a/solution.py
+++ b/solution.py
@@ -74,7 +74,7 @@
     return lax.dot_general(a, b, (((0,), (0,)), ((), ())), preferred_element_type=jnp.float32)
 
 
-CHUNKS = 2
+CHUNKS = 4
 PART = SLOT // CHUNKS
 PAIRS = PART // 2
 BLOCKS = 3 * PART + PAIRS
@@ -234,7 +234,7 @@
     place_in_side = lane % SIDE
 
     def ahead(h):
-        return 1 if h == 0 else 3
+        return 1 if h % 2 == 0 else 3
 
     def a_device(step):
         return plane_device((a_here + step) % 4, b_here)
@@ -443,7 +443,7 @@
             jax.ShapeDtypeStruct((NGRAN,), jnp.int32),
         ),
         in_specs=[smem, smem, smem, smem, hbm, hbm, hbm],
-        out_specs=(hbm, hbm, hbm, smem),
+        out_specs=(hbm, hbm, pl.BlockSpec(memory_space=pltpu.VMEM), smem),
         scratch_shapes=[
             pltpu.VMEM((32, 32, DC), jnp.bfloat16),
             pltpu.VMEM((EXPERTS, 32, DC), jnp.bfloat16),

time: 164 us -> 159 us (0.970)
  Pallas kernels: 161 us -> 154 us
    pallas_call x1, Pallas kernels: 104 us -> 99.4 us  [rows_and_hidden(): pl.pallas_call(rows_kernel, out_shape=(jax.ShapeDtypeStruct((X, SLOT, Y,...]
    pallas_call x1, Pallas kernels: 49.1 us -> 45.8 us  [reduce_grads(): pl.pallas_call(reduce_kernel, out_shape=jax.ShapeDtypeStruct((EXPERTS, 3,...]
where the time goes in v6:
time: 159 us; the launch traced here: 157 us
  Pallas kernels  154 us (97%)
  local copies, waits for them, and re-layouts  3.05 us (2%)
    pallas_call x1, Pallas kernels, rows_and_hidden(): pl.pallas_call(rows_kernel, out_shape=(jax.ShapeDtypeStruct((X, SLOT, Y,...  99.4 us
    pallas_call x1, Pallas kernels, reduce_grads(): pl.pallas_call(reduce_kernel, out_shape=jax.ShapeDtypeStruct((EXPERTS, 3,...  45.8 us
    pallas_call x1, Pallas kernels, gradients(): pl.pallas_call(grads_kernel, out_shape=jax.ShapeDtypeStruct((EXPERTS, GRO...  9.16 us

profile of v6, /device:TPU:25, one launch (start us, length us, event | category | flops | bytes accessed | tf_op | source)
XLA Modules:
  0.0 157.4 jit_solution(13834317995757549778)
XLA Ops:
  0.0 1.4 copy.8.dest
  1.4 99.4 %rows_and_hidden.1 = (bf16[4,8,4,16,384]{4,3,2,1,0:T(8,128)(2,1)}, bf16[4,8,4,16,384]{4,3,2,1,0:T(8,128)(2,1)}, bf16[4,4,4,7,16,128]{5,4,3,2,1,0:T(8,128)(2,1)}, s32[32]{0:T(128)}) custom-call(s32[8]{0:T(128)} %counts.1, s32[32]{0:T(128)} %column.1, s32[32,8]{1,0:T(8,128)} %copy.8.dest, s32[32]{0:T(128)} %live.1, bf16[8,16,6144]{2,1,0:T(8,128)(2,1)} %tok.1, ...), custom_call_target="tpu_custom_call" | custom-call | tf_op jit(solution)/shard_map/rows_and_hidden/pallas_call | solution.py:437
  100.7 9.2 %gradients.1.grads = bf16[8,448,384]{2,1,0:T(8,128)(2,1)} custom-call(s32[32]{0:T(128)} %get-tuple-element.9.gexp, bf16[32,64,384]{2,1,0:T(8,128)(2,1)} %bitcast.2, bf16[32,64,384]{2,1,0:T(8,128)(2,1)} %bitcast.3, bf16[4,4,4,7,16,128]{5,4,3,2,1,0:T(8,128)(2,1)} %get-tuple-element.12.hg), custom_call_target="tpu_custom_call" | custom-call | tf_op jit(solution)/shard_map/gradients/pallas_call | solution.py:573
  109.9 45.8 %reduce_grads.1 = bf16[8,3,18,192]{3,2,1,0:T(8,128)(2,1)} custom-call(bf16[8,448,384]{2,1,0:T(8,128)(2,1)} %gradients.1.grads), custom_call_target="tpu_custom_call" | custom-call | tf_op jit(solution)/shard_map/reduce_grads/pallas_call | solution.py:775
  155.7 1.7 %copy.9 = bf16[8,3,18,192]{3,0,2,1:T(8,128)(2,1)} copy(bf16[8,3,18,192]{3,2,1,0:T(8,128)(2,1)} %reduce_grads.1) | data formatting | bytes 331776 | tf_op jit(solution)/shard_map/reduce_grads/pallas_call | solution.py:775

commit v7 on v6

--- a/solution.py
+++ b/solution.py
@@ -83,7 +83,7 @@
 
 
 def rows_kernel(
-    counts, column, dest, live, tok, cot, wts, xg, qg, hg, gexp, wr, sel, wg, xv, qv, p1, m1, r1, s2, r2, hid, xs_sem, xr_sem, qs_sem, qr_sem,
+    counts, column, dest, live, tok, cot, wts, xg, qg, hg, gexp, wr, sel, wg, xv, qv, p1, m1, r1, n1, rn, s2, r2, hid, xs_sem, xr_sem, qs_sem, qr_sem,
     ws_sem, wr_sem, own_sem, rs_sem, rr_sem, ls_sem, lr_sem, ss_sem, sr_sem, p1s_sem, p1r_sem, p2s_sem, p2r_sem,
     has_sem, har_sem, hbs_sem, hbr_sem, keep_sem,
 ):
@@ -127,28 +127,29 @@
             ).start()
         return carry
 
+    def columns(ref, px, py):
+        return ref.at[:, :, pl.ds(pl.multiple_of((px * Y + py) * DC, 128), DC)]
+
+    def x_copy(step):
+        px, py = plane_peer(x, y, step)
+        return remote(
+            columns(tok, px, py), xv.at[x, :, y], xs_sem.at[step], xr_sem.at[step], device(px, py, z, k)
+        )
+
+    def q_copy(step):
+        px, py = plane_peer(x, y, step)
+        return remote(
+            columns(cot, px, py), qv.at[x, :, y], qs_sem.at[step], qr_sem.at[step], device(px, py, z, k)
+        )
+
+    for step in range(5):
+        x_copy(step).start()
     lax.fori_loop(1, 32, send_weights, 0)
     for part in range(2):
         pltpu.make_async_copy(
             weight_piece(me_col, part), wr.at[me_col, pl.ds(part * 16, 16), :], wr_sem
         ).start()
-
-    def columns(ref, px, py):
-        return ref.at[:, :, pl.ds(pl.multiple_of((px * Y + py) * DC, 128), DC)]
-
-    def x_copy(step):
-        px, py = plane_peer(x, y, step)
-        return remote(
-            columns(tok, px, py), xv.at[x, :, y], xs_sem.at[step], xr_sem.at[step], device(px, py, z, k)
-        )
-
-    def q_copy(step):
-        px, py = plane_peer(x, y, step)
-        return remote(
-            columns(cot, px, py), qv.at[x, :, y], qs_sem.at[step], qr_sem.at[step], device(px, py, z, k)
-        )
-
-    for step in range(GROUP - 1):
+    for step in range(5, GROUP - 1):
         x_copy(step).start()
     own_x = pltpu.make_async_copy(columns(tok, x, y), xv.at[x, :, y], own_sem.at[0])
     own_q = pltpu.make_async_copy(columns(cot, x, y), qv.at[x, :, y], own_sem.at[1])
@@ -242,18 +243,18 @@
     def b_device(step):
         return plane_device(a_here, (b_here + step) % 4)
 
-    def first_copy(h, kind, src, step):
+    def first_copy(h, kind, src, dst, step):
         at = h * 3 + kind
-        return remote(src, r1.at[h, kind], p1s_sem.at[at], p1r_sem.at[at], a_device(step))
+        return remote(src, dst, p1s_sem.at[at], p1r_sem.at[at], a_device(step))
 
     def far_copy(h):
-        return first_copy(h, 0, p1.at[(a_here + 2) % 4, h], ahead(h))
+        return first_copy(h, 0, n1.at[h, 0], rn.at[h, 0], ahead(h))
 
     def sum_copy(h):
-        return first_copy(h, 1, m1.at[h], ahead(h))
+        return first_copy(h, 1, m1.at[h], r1.at[h], ahead(h))
 
     def near_copy(h):
-        return first_copy(h, 2, p1.at[(a_here + 4 - ahead(h)) % 4, h], 4 - ahead(h))
+        return first_copy(h, 2, n1.at[h, 1], rn.at[h, 1], 4 - ahead(h))
 
     def second_copy(h, j):
         b = (b_here + j) % 4
@@ -334,6 +335,13 @@
             return carry
 
         lax.fori_loop(0, X * PAIRS, project_q, 0)
+
+        def narrow(b, carry):
+            n1[h, 0, b] = p1[(a_here + 2) % 4, h, b].astype(jnp.bfloat16)
+            n1[h, 1, b] = p1[(a_here + 4 - ahead(h)) % 4, h, b].astype(jnp.bfloat16)
+            return carry
+
+        lax.fori_loop(0, 4, narrow, 0)
         far_copy(h).start()
         near_copy(h).start()
 
@@ -341,7 +349,7 @@
         far_copy(h).wait_recv()
 
         def relay(b, carry):
-            m1[h, b] = p1[(a_here + ahead(h)) % 4, h, b] + r1[h, 0, b]
+            m1[h, b] = p1[(a_here + ahead(h)) % 4, h, b] + rn[h, 0, b].astype(jnp.float32)
             return carry
 
         lax.fori_loop(0, 4, relay, 0)
@@ -352,7 +360,7 @@
         sum_copy(h).wait_recv()
 
         def sum_first(b, carry):
-            s2[b, h] = p1[a_here, h, b] + r1[h, 1, b] + r1[h, 2, b]
+            s2[b, h] = p1[a_here, h, b] + r1[h, b] + rn[h, 1, b].astype(jnp.float32)
             return carry
 
         lax.fori_loop(0, 4, sum_first, 0)
@@ -432,7 +440,8 @@
     dma = pltpu.SemaphoreType.DMA
     spread = pltpu.VMEM((X, SLOT, Y, ROWS, DC), jnp.bfloat16)
     sums = pltpu.VMEM((4, CHUNKS, 4, BLOCKS, ROWS, MAIN), SUM_TYPE)
-    arrived = pltpu.VMEM((CHUNKS, 3, 4, BLOCKS, ROWS, MAIN), SUM_TYPE)
+    relayed = pltpu.VMEM((CHUNKS, 4, BLOCKS, ROWS, MAIN), SUM_TYPE)
+    narrow = pltpu.VMEM((CHUNKS, 2, 4, BLOCKS, ROWS, MAIN), jnp.bfloat16)
     halfway = pltpu.VMEM((4, CHUNKS, BLOCKS, ROWS, MAIN), jnp.float32)
     return pl.pallas_call(
         rows_kernel,
@@ -451,8 +460,10 @@
             spread,
             spread,
             sums,
-            pltpu.VMEM((CHUNKS, 4, BLOCKS, ROWS, MAIN), SUM_TYPE),
-            arrived,
+            relayed,
+            relayed,
+            narrow,
+            narrow,
             halfway,
             halfway,
             pltpu.VMEM((CHUNKS, BLOCKS, ROWS, MAIN), jnp.bfloat16),

time: 159 us -> 154 us (0.969)
  Pallas kernels: 154 us -> 151 us
    pallas_call x1, Pallas kernels: 99.4 us -> 94.7 us  [rows_and_hidden(): pl.pallas_call(rows_kernel, out_shape=(jax.ShapeDtypeStruct((X, SLOT, Y,...]
    pallas_call x1, Pallas kernels: 45.8 us -> 48 us  [reduce_grads(): pl.pallas_call(reduce_kernel, out_shape=jax.ShapeDtypeStruct((EXPERTS, 3,...]
where the time goes in v7:
time: 154 us
  Pallas kernels  151 us (98%)
  local copies, waits for them, and re-layouts  3.05 us (2%)
    pallas_call x1, Pallas kernels, rows_and_hidden(): pl.pallas_call(rows_kernel, out_shape=(jax.ShapeDtypeStruct((X, SLOT, Y,...  94.7 us
    pallas_call x1, Pallas kernels, reduce_grads(): pl.pallas_call(reduce_kernel, out_shape=jax.ShapeDtypeStruct((EXPERTS, 3,...  48 us
    pallas_call x1, Pallas kernels, gradients(): pl.pallas_call(grads_kernel, out_shape=jax.ShapeDtypeStruct((EXPERTS, GRO...  7.95 us

profile of v7, /device:TPU:25, one launch (start us, length us, event | category | flops | bytes accessed | tf_op | source)
XLA Modules:
  0.0 153.8 jit_solution(5865337756506640432)
XLA Ops:
  0.0 1.4 copy.8.dest
  1.4 94.7 %rows_and_hidden.1 = (bf16[4,8,4,16,384]{4,3,2,1,0:T(8,128)(2,1)}, bf16[4,8,4,16,384]{4,3,2,1,0:T(8,128)(2,1)}, bf16[4,4,4,7,16,128]{5,4,3,2,1,0:T(8,128)(2,1)}, s32[32]{0:T(128)}) custom-call(s32[8]{0:T(128)} %counts.1, s32[32]{0:T(128)} %column.1, s32[32,8]{1,0:T(8,128)} %copy.8.dest, s32[32]{0:T(128)} %live.1, bf16[8,16,6144]{2,1,0:T(8,128)(2,1)} %tok.1, ...), custom_call_target="tpu_custom_call" | custom-call | tf_op jit(solution)/shard_map/rows_and_hidden/pallas_call | solution.py:446
  96.1 7.9 %gradients.1.grads = bf16[8,448,384]{2,1,0:T(8,128)(2,1)} custom-call(s32[32]{0:T(128)} %get-tuple-element.9.gexp, bf16[32,64,384]{2,1,0:T(8,128)(2,1)} %bitcast.2, bf16[32,64,384]{2,1,0:T(8,128)(2,1)} %bitcast.3, bf16[4,4,4,7,16,128]{5,4,3,2,1,0:T(8,128)(2,1)} %get-tuple-element.12.hg), custom_call_target="tpu_custom_call" | custom-call | tf_op jit(solution)/shard_map/gradients/pallas_call | solution.py:584
  104.0 48.0 %reduce_grads.1 = bf16[8,3,18,192]{3,2,1,0:T(8,128)(2,1)} custom-call(bf16[8,448,384]{2,1,0:T(8,128)(2,1)} %gradients.1.grads), custom_call_target="tpu_custom_call" | custom-call | tf_op jit(solution)/shard_map/reduce_grads/pallas_call | solution.py:786
  152.1 1.7 %copy.9 = bf16[8,3,18,192]{3,0,2,1:T(8,128)(2,1)} copy(bf16[8,3,18,192]{3,2,1,0:T(8,128)(2,1)} %reduce_grads.1) | data formatting | bytes 331776 | tf_op jit(solution)/shard_map/reduce_grads/pallas_call | solution.py:786

commit v8 on v7

--- a/solution.py
+++ b/solution.py
@@ -497,7 +497,7 @@
     )(counts, column, dest, live, tok, cot, wts)
 
 
-def grads_kernel(gexp, xg, qg, hg, out, xs, qs, hs, acc, rounded, source, rank, ends, in_sem, out_sem):
+def grads_kernel(gexp, xg, qg, hg, out, xs, qs, hs, acc, source, rank, ends, in_sem, out_sem):
     loads = [
         pltpu.make_async_copy(ref, held, in_sem.at[i]) for i, (ref, held) in enumerate(((hg, hs), (xg, xs), (qg, qs)))
     ]
@@ -566,14 +566,13 @@
 
         end = ends[e]
         lax.fori_loop(start, end, tile_step, 0)
-        rounded[e] = acc[e].astype(jnp.bfloat16)
-        pltpu.make_async_copy(rounded.at[e], out.at[e], out_sem.at[e]).start()
+        pltpu.make_async_copy(acc.at[e], out.at[e], out_sem.at[e]).start()
         return end
 
     lax.fori_loop(0, EXPERTS, expert_step, 0)
 
     def finish(e, carry):
-        pltpu.make_async_copy(rounded.at[e], out.at[e], out_sem.at[e]).wait()
+        pltpu.make_async_copy(acc.at[e], out.at[e], out_sem.at[e]).wait()
         return carry
 
     lax.fori_loop(0, EXPERTS, finish, 0)
@@ -583,7 +582,7 @@
     hbm = pl.BlockSpec(memory_space=pl.ANY)
     return pl.pallas_call(
         grads_kernel,
-        out_shape=jax.ShapeDtypeStruct((EXPERTS, GROWS, DC), jnp.bfloat16),
+        out_shape=jax.ShapeDtypeStruct((EXPERTS, GROWS, DC), jnp.float32),
         in_specs=[pl.BlockSpec(memory_space=pltpu.SMEM), hbm, hbm, hbm],
         out_specs=hbm,
         scratch_shapes=[
@@ -591,7 +590,6 @@
             pltpu.VMEM(qg.shape, jnp.bfloat16),
             pltpu.VMEM(hg.shape, jnp.bfloat16),
             pltpu.VMEM((EXPERTS, GROWS, DC), jnp.float32),
-            pltpu.VMEM((EXPERTS, GROWS, DC), jnp.bfloat16),
             pltpu.SMEM((MAX_TILES * PER_TILE,), jnp.int32),
             pltpu.SMEM((NGRAN,), jnp.int32),
             pltpu.SMEM((EXPERTS + 1,), jnp.int32),
@@ -669,7 +667,7 @@
             ready.add(off)
         e = (z + off + Z) % Z
         cut = slice(j * QUART, (j + 1) * QUART)
-        return own[e, cut].astype(jnp.float32) + sib[e, cut].astype(jnp.float32)
+        return own[e, cut] + sib[e, cut]
 
     chain = {}
     for dist in (4, 3, 2, 1):
@@ -781,7 +779,7 @@
 
 def reduce_grads(grads):
     dma = pltpu.SemaphoreType.DMA
-    wide = pltpu.VMEM((EXPERTS, HALF, DC), jnp.bfloat16)
+    wide = pltpu.VMEM((EXPERTS, HALF, DC), jnp.float32)
     steps = pltpu.VMEM((2, 2, 4, QUART, DC), jnp.bfloat16)
     return pl.pallas_call(
         reduce_kernel,

time: 154 us -> 154 us (level)
  no operation moved by 1% of the time
where the time goes in v8:
time: 154 us; the launch traced here: 153 us
  Pallas kernels  150 us (97%)
  local copies, waits for them, and re-layouts  3.05 us (2%)
    pallas_call x1, Pallas kernels, rows_and_hidden(): pl.pallas_call(rows_kernel, out_shape=(jax.ShapeDtypeStruct((X, SLOT, Y,...  94.8 us
    pallas_call x1, Pallas kernels, reduce_grads(): pl.pallas_call(reduce_kernel, out_shape=jax.ShapeDtypeStruct((EXPERTS, 3,...  47.9 us
    pallas_call x1, Pallas kernels, gradients(): pl.pallas_call(grads_kernel, out_shape=jax.ShapeDtypeStruct((EXPERTS, GRO...  7.37 us

profile of v8, /device:TPU:25, one launch (start us, length us, event | category | flops | bytes accessed | tf_op | source)
XLA Modules:
  0.0 153.1 jit_solution(8630166166203683046)
XLA Ops:
  0.0 1.4 copy.8.dest
  1.4 94.8 %rows_and_hidden.1 = (bf16[4,8,4,16,384]{4,3,2,1,0:T(8,128)(2,1)}, bf16[4,8,4,16,384]{4,3,2,1,0:T(8,128)(2,1)}, bf16[4,4,4,7,16,128]{5,4,3,2,1,0:T(8,128)(2,1)}, s32[32]{0:T(128)}) custom-call(s32[8]{0:T(128)} %counts.1, s32[32]{0:T(128)} %column.1, s32[32,8]{1,0:T(8,128)} %copy.8.dest, s32[32]{0:T(128)} %live.1, bf16[8,16,6144]{2,1,0:T(8,128)(2,1)} %tok.1, ...), custom_call_target="tpu_custom_call" | custom-call | tf_op jit(solution)/shard_map/rows_and_hidden/pallas_call | solution.py:446
  96.1 7.4 %gradients.1.grads = f32[8,448,384]{2,1,0:T(8,128)} custom-call(s32[32]{0:T(128)} %get-tuple-element.9.gexp, bf16[32,64,384]{2,1,0:T(8,128)(2,1)} %bitcast.2, bf16[32,64,384]{2,1,0:T(8,128)(2,1)} %bitcast.3, bf16[4,4,4,7,16,128]{5,4,3,2,1,0:T(8,128)(2,1)} %get-tuple-element.12.hg), custom_call_target="tpu_custom_call" | custom-call | tf_op jit(solution)/shard_map/gradients/pallas_call | solution.py:583
  103.5 47.9 %reduce_grads.1 = bf16[8,3,18,192]{3,2,1,0:T(8,128)(2,1)} custom-call(f32[8,448,384]{2,1,0:T(8,128)} %gradients.1.grads), custom_call_target="tpu_custom_call" | custom-call | tf_op jit(solution)/shard_map/reduce_grads/pallas_call | solution.py:784
  151.5 1.7 %copy.9 = bf16[8,3,18,192]{3,0,2,1:T(8,128)(2,1)} copy(bf16[8,3,18,192]{3,2,1,0:T(8,128)(2,1)} %reduce_grads.1) | data formatting | bytes 331776 | tf_op jit(solution)/shard_map/reduce_grads/pallas_call | solution.py:784

commit v9 on v8

--- a/solution.py
+++ b/solution.py
@@ -398,16 +398,21 @@
             hidden_near(h, 0, step).start()
         hidden_keep(h).start()
 
-    arrivals = (0, 1, 3, 2)
-    for n, j in enumerate(arrivals):
-        if n + 1 < len(arrivals):
-            for h in range(CHUNKS):
-                hidden_first(h, arrivals[n + 1]).wait_recv()
-                for step in (1, 3):
-                    hidden_near(h, arrivals[n + 1], step).start()
-        for h in range(CHUNKS):
-            hidden_near(h, j, ahead(h)).wait_recv()
-            hidden_far(h, j).start()
+    def pass_on(h, j):
+        hidden_first(h, j).wait_recv()
+        for step in (1, 3):
+            hidden_near(h, j, step).start()
+
+    def pass_far(h, j):
+        hidden_near(h, j, ahead(h)).wait_recv()
+        hidden_far(h, j).start()
+
+    for h in range(CHUNKS):
+        for j in (1, 3, 2):
+            pass_on(h, j)
+    for h in range(CHUNKS):
+        for j in (0, 1, 3, 2):
+            pass_far(h, j)
     for h in range(CHUNKS):
         for j in range(4):
             hidden_near(h, j, 4 - ahead(h)).wait_recv()
@@ -758,7 +763,7 @@
 
         return carry
 
-    lax.fori_loop(0, 8, start, 0)
+    lax.fori_loop(0, 8, lambda i, carry: start((i + z) % 8, carry), 0)
     lax.fori_loop(0, 8, finish_send, 0)
     def unpack(e, carry):
         value = got[e].astype(jnp.float32)

time: 154 us -> 151 us (0.981)
  Pallas kernels: 150 us -> 148 us
    pallas_call x1, Pallas kernels: 47.9 us -> 45.9 us  [reduce_grads(): pl.pallas_call(reduce_kernel, out_shape=jax.ShapeDtypeStruct((EXPERTS, 3,...]
where the time goes in v9:
time: 151 us
  Pallas kernels  148 us (98%)
  local copies, waits for them, and re-layouts  3.05 us (2%)
    pallas_call x1, Pallas kernels, rows_and_hidden(): pl.pallas_call(rows_kernel, out_shape=(jax.ShapeDtypeStruct((X, SLOT, Y,...  94.1 us
    pallas_call x1, Pallas kernels, reduce_grads(): pl.pallas_call(reduce_kernel, out_shape=jax.ShapeDtypeStruct((EXPERTS, 3,...  45.9 us
    pallas_call x1, Pallas kernels, gradients(): pl.pallas_call(grads_kernel, out_shape=jax.ShapeDtypeStruct((EXPERTS, GRO...  7.78 us

profile of v9, /device:TPU:25, one launch (start us, length us, event | category | flops | bytes accessed | tf_op | source)
XLA Modules:
  0.0 150.9 jit_solution(15216076921694664240)
XLA Ops:
  0.0 1.4 copy.8.dest
  1.4 94.1 %rows_and_hidden.1 = (bf16[4,8,4,16,384]{4,3,2,1,0:T(8,128)(2,1)}, bf16[4,8,4,16,384]{4,3,2,1,0:T(8,128)(2,1)}, bf16[4,4,4,7,16,128]{5,4,3,2,1,0:T(8,128)(2,1)}, s32[32]{0:T(128)}) custom-call(s32[8]{0:T(128)} %counts.1, s32[32]{0:T(128)} %column.1, s32[32,8]{1,0:T(8,128)} %copy.8.dest, s32[32]{0:T(128)} %live.1, bf16[8,16,6144]{2,1,0:T(8,128)(2,1)} %tok.1, ...), custom_call_target="tpu_custom_call" | custom-call | tf_op jit(solution)/shard_map/rows_and_hidden/pallas_call | solution.py:451
  95.5 7.8 %gradients.1.grads = f32[8,448,384]{2,1,0:T(8,128)} custom-call(s32[32]{0:T(128)} %get-tuple-element.9.gexp, bf16[32,64,384]{2,1,0:T(8,128)(2,1)} %bitcast.2, bf16[32,64,384]{2,1,0:T(8,128)(2,1)} %bitcast.3, bf16[4,4,4,7,16,128]{5,4,3,2,1,0:T(8,128)(2,1)} %get-tuple-element.12.hg), custom_call_target="tpu_custom_call" | custom-call | tf_op jit(solution)/shard_map/gradients/pallas_call | solution.py:588
  103.3 45.9 %reduce_grads.1 = bf16[8,3,18,192]{3,2,1,0:T(8,128)(2,1)} custom-call(f32[8,448,384]{2,1,0:T(8,128)} %gradients.1.grads), custom_call_target="tpu_custom_call" | custom-call | tf_op jit(solution)/shard_map/reduce_grads/pallas_call | solution.py:789
  149.2 1.7 %copy.9 = bf16[8,3,18,192]{3,0,2,1:T(8,128)(2,1)} copy(bf16[8,3,18,192]{3,2,1,0:T(8,128)(2,1)} %reduce_grads.1) | data formatting | bytes 331776 | tf_op jit(solution)/shard_map/reduce_grads/pallas_call | solution.py:789
